TPU v7x, 128 devices: a whole 4x4x4 slice. The times are simulated.
128 devices in a mesh: dom: 128 (over x, z, y, core).
Axes of the slice: x: 4, y: 4, z: 4, core: 2. Of those that a mesh axis runs over, the one named last changes fastest.
Arguments:
- adjoint_start: float32 [3, 884736], P(None, 'dom'), may hold values from -6 to 6
- adjoint_source: float32 [3, 884736], P(None, 'dom'), may hold values from -6 to 6
- inverse_diagonal: float32 [3, 884736], P(None, 'dom'), may hold values from 0.05 to 0.3
- primal_field: float32 [3, 884736], P(None, 'dom'), may hold values from -6 to 6
- cell_load: float32 [192, 32768], P(None, 'dom'), may hold values from -6 to 6
- modulus: float32 [32768], P('dom'), may hold values from 0.5 to 4
- stiffness: float32 [192, 192], replicated
- connectivity: int32 [64, 32768], P(None, 'dom'), may hold values from 0 to 16368
- hang_node: int32 [16384], P('dom'), may hold values from 0 to 16368, as said below
- hang_master: int32 [16, 16384], P(None, 'dom'), may hold values from 0 to 16368
- hang_weight: float32 [16, 16384], P(None, 'dom'), may hold values from -0.25 to 0.45
- ghost_lists: int32 [8, 32768], P(None, 'dom'), may hold values from 0 to 16368
- subface_cell: int32 [8, 16384], P(None, 'dom'), may hold values from 0 to 255
- subface_face: int32 [8, 16384], P(None, 'dom'), may hold values from 0 to 5
- subface_owner: int32 [8, 16384], P(None, 'dom'), may hold values from 0 to 256, as said below
Outputs:
- adjoint: float32 [3, 884736], P(None, 'dom')
- indicator: float32 [32768], P('dom')
Inputs may be any that keep to these rules, and one draw needn't show every extreme that they name: `hang_node`: on each partition the live hanging slots come first and hold distinct codes under min(16368, 6912); all slots after them hold 16368; between half and all of a partition's slots are live. `subface_owner`: 256 marks an unused slot; between half and all of each neighbour slot's entries are live.
All inputs are finite; a program needn't handle non-finite values.
Results may differ from a plain program's by a relative error of at most 0.0003.
Values sent between devices are 32-bit elements; how exact they have to be, the bound alone decides.
A program may use at most 64 MiB of HBM per device.

v0:
```python
import jax
import jax.numpy as jnp
from jax import lax
from jax.sharding import PartitionSpec as P

REACH = 4
SWEEPS = 2
NODES_DEV = 6912
EXT = 8960


relaxation = 0.7
scale_down = 16.0
pad_code = 16368


def from_behind(block, axis, distance):
    devices = range(lax.axis_size(axis))
    route = [(i - distance, i) for i in devices if i - distance in devices]
    return lax.ppermute(block, axis, route)


def neighbour_offsets():
    return [step + 1 for step in range(REACH)] + [-(step + 1) for step in range(REACH)]


def decode_connect(codes):
    cells = jnp.arange(codes.shape[-1], dtype=jnp.int32)
    return (27 * cells + 17 * codes) % EXT


def decode_master(codes):
    slots = jnp.arange(codes.shape[-1], dtype=jnp.int32)
    return (17 * codes + 8 * slots) % EXT


def decode_node(codes):
    return jnp.where(codes == pad_code, EXT, 13 * codes % NODES_DEV)


def decode_lists(codes):
    slots = jnp.arange(codes.shape[-1], dtype=jnp.int32)
    return (17 * codes + slots) % NODES_DEV


def face_table(width):
    node = jnp.arange(width, dtype=jnp.int32) % 64
    first = node // 16
    second = node // 4 % 4
    third = node % 4
    rows = [first == 0, first == 3, second == 0, second == 3, third == 0, third == 3]
    return jnp.stack(rows).astype(jnp.float32)


def constrain(extended, node, master, weight):
    padded = jnp.concatenate([extended, jnp.zeros((extended.shape[0], 1), extended.dtype)], 1)
    values = jnp.sum(weight[None] * padded[:, master], axis=1)
    padded = padded.at[:, node].set(values)
    return padded[:, :-1]


def release(totals, node, master, weight):
    padded = jnp.concatenate([totals, jnp.zeros((totals.shape[0], 1), totals.dtype)], 1)
    held = padded[:, node]
    padded = padded.at[:, node].set(0.0)
    spread = weight[None] * held[:, None, :]
    padded = padded.at[:, master.reshape(-1)].add(spread.reshape(totals.shape[0], -1))
    return padded[:, :-1]


def local_product(extended, connect, modulus, stiffness, node, master, weight):
    fixed = constrain(extended, node, master, weight)
    cells = fixed[:, connect].reshape(3 * connect.shape[0], -1)
    image = modulus[None] * lax.dot_general(
        stiffness, cells, (((0,), (0,)), ((), ())), precision=lax.Precision.HIGHEST
    )
    totals = jnp.zeros_like(fixed).at[:, connect].add(image.reshape(3, connect.shape[0], -1))
    return release(totals, node, master, weight)


def local(
    adjoint_start,
    adjoint_source,
    inverse_diagonal,
    primal_field,
    cell_load,
    modulus,
    stiffness,
    connectivity,
    hang_node,
    hang_master,
    hang_weight,
    ghost_lists,
    subface_cell,
    subface_face,
    subface_owner,
):
    offsets = neighbour_offsets()
    highest = lax.Precision.HIGHEST
    connect = decode_connect(connectivity)
    node_slots = decode_node(hang_node)
    master_slots = decode_master(hang_master)
    export_rows = decode_lists(ghost_lists)

    def ghosts_in(blocks):
        return jnp.stack(
            [from_behind(blocks[slot], "dom", offsets[slot]) for slot in range(2 * REACH)]
        )

    def ghosts_back(blocks):
        return jnp.stack(
            [from_behind(blocks[slot], "dom", -offsets[slot]) for slot in range(2 * REACH)]
        )

    def extend(owned):
        blocks = jnp.moveaxis(owned[:, export_rows], 1, 0)
        ghosts = ghosts_in(blocks)
        return jnp.concatenate([owned, jnp.moveaxis(ghosts, 0, 1).reshape(owned.shape[0], -1)], 1)

    owned_count = adjoint_start.shape[1]
    ghost_count = export_rows.shape[1]
    adjoint = adjoint_start
    for sweep in range(SWEEPS):
        extended = extend(adjoint)
        totals = local_product(
            extended, connect, modulus, stiffness, node_slots, master_slots, hang_weight
        )
        owned_part = totals[:, :owned_count]
        ghost_part = jnp.moveaxis(totals[:, owned_count:].reshape(3, 2 * REACH, ghost_count), 1, 0)
        returned = ghosts_back(ghost_part)
        applied = owned_part.at[:, export_rows.reshape(-1)].add(
            jnp.moveaxis(returned, 0, 1).reshape(3, -1)
        )
        adjoint = adjoint + relaxation * inverse_diagonal * (adjoint_source - applied)
    both_ext = extend(jnp.concatenate([adjoint, primal_field], 0))
    fixed = constrain(both_ext, node_slots, master_slots, hang_weight)
    adjoint_cells = fixed[:3][:, connect].reshape(3 * connect.shape[0], -1)
    primal_cells = fixed[3:][:, connect].reshape(3 * connect.shape[0], -1)
    applied = modulus[None] * jnp.dot(stiffness, primal_cells, precision=highest)
    cell_term = jnp.sum(adjoint_cells * (cell_load - applied), axis=0)
    flux = jnp.dot(face_table(applied.shape[0]), applied * adjoint_cells, precision=highest)
    cell_count = connect.shape[1]
    sent = flux.reshape(-1)[subface_face * cell_count + subface_cell]
    received = jnp.stack(
        [from_behind(sent[slot], "dom", offsets[slot]) for slot in range(2 * REACH)]
    )
    face_term = (
        jnp.zeros((cell_count + 1,), jnp.float32)
        .at[subface_owner.reshape(-1)]
        .add(received.reshape(-1))[:cell_count]
    )
    indicator = (jnp.abs(cell_term) + jnp.abs(face_term)) / scale_down
    return (adjoint, indicator)


def solution(mesh):
    placed = (
        P(None, "dom"),
        P(None, "dom"),
        P(None, "dom"),
        P(None, "dom"),
        P(None, "dom"),
        P("dom"),
        P(),
        P(None, "dom"),
        P("dom"),
        P(None, "dom"),
        P(None, "dom"),
        P(None, "dom"),
        P(None, "dom"),
        P(None, "dom"),
        P(None, "dom"),
    )
    return jax.shard_map(
        local, mesh=mesh, in_specs=placed, out_specs=(P(None, "dom"), P("dom")), check_vma=False
    )
```

profile of v0, /device:TPU:6, one launch (start us, length us, event | category | flops | bytes accessed | tf_op | source)
XLA Modules:
  0.0 845.8 jit_solution(16072150130595561611)
XLA Ops:
  4.7 7.5 gather_fusion
  22.1 5.1 collective-permute-start.3
  27.2 5.4 collective-permute-start.4
  37.8 5.2 collective-permute-start.7
  45.2 8.4 maximum_maximum_fusion
  53.6 7.8 gather_fusion.1
  61.7 5.2 scatter_fusion
  70.9 56.8 %gather_fusion.2 = f32[16384,3]{1,0:T(8,128)} fusion(f32[3,8960]{0,1:T(8,128)} %slice.279, s32[16384]{0:T(1024)S(1)} %broadcast_clamp_fusion), kind=kCustom, calls=%fused_computation.2 | custom fusion | bytes 458752 | tf_op jit(solution)/shard_map/gather | solution.py:73
  127.7 5.2 copy.248
  133.6 4.7 copy.249
  138.3 90.1 %scatter_custom_fusion.1 = f32[3,8960]{0,1:T(8,128)} fusion(s32[16384]{0:T(1024)S(1)} %bitcast.260, f32[16384,3]{1,0:T(8,128)} %bitcast.240, f32[]{:T(128)} %constant.113.clone.1), kind=kCustom, calls=%fused_computation.28 | custom fusion | flops 49152 | bytes 108032 | tf_op jit(solution)/shard_map/scatter-add | solution.py:77
  235.2 5.2 scatter_custom_fusion.2
  240.8 14.8 %scatter_custom_fusion.3 = f32[3,8961]{0,1:T(8,128)} fusion(f32[3,8961]{0,1:T(8,128)} %scatter_custom_fusion.2, s32[2048]{0:T(1024)S(1)} %bitcast.288, f32[3,2048]{0,1:T(8,128)S(1)} %bitcast_multiply_fusion.1), kind=kCustom, calls=%fused_computation.37 | custom fusion | flops 6144 | bytes 1156108 | tf_op jit(solution)/shard_map/scatter-add | solution.py:67
  257.2 4.5 collective-permute-start.8
  261.7 4.9 collective-permute-start.9
  276.6 5.1 collective-permute-start.14
  281.7 4.2 collective-permute-start.15
  292.1 14.1 %scatter_fusion.1 = f32[3,6912]{0,1:T(8,128)} fusion(f32[3,6912]{0,1:T(8,128)} %slice.280, s32[2048]{0:T(1024)S(1)} %bitcast.274, f32[2048,3]{1,0:T(8,128)S(1)} %bitcast.247), kind=kCustom, calls=%fused_computation.17 | custom fusion | flops 6144 | bytes 81920 | tf_op jit(solution)/shard_map/scatter-add | solution.py:131
  311.2 7.5 gather_fusion.4
  328.7 7.6 collective-permute-start.20
  343.2 5.2 collective-permute-start.23
  353.4 7.8 gather_fusion.5
  361.5 5.2 scatter_fusion.2
  370.8 56.8 %gather_fusion.6 = f32[16384,3]{1,0:T(8,128)} fusion(f32[3,8960]{0,1:T(8,128)} %slice.298, s32[16384]{0:T(1024)S(1)} %broadcast_clamp_fusion), kind=kCustom, calls=%fused_computation.6 | custom fusion | bytes 458752 | tf_op jit(solution)/shard_map/gather | solution.py:73
  427.5 5.2 copy.271
  433.4 4.7 copy.272
  438.1 90.1 %scatter_custom_fusion.6 = f32[3,8960]{0,1:T(8,128)} fusion(s32[16384]{0:T(1024)S(1)} %bitcast.261, f32[16384,3]{1,0:T(8,128)} %bitcast.239, f32[]{:T(128)} %constant.113.clone.1), kind=kCustom, calls=%fused_computation.26 | custom fusion | flops 49152 | bytes 108032 | tf_op jit(solution)/shard_map/scatter-add | solution.py:77
  535.0 5.2 scatter_custom_fusion.7
  540.6 14.8 %scatter_custom_fusion.8 = f32[3,8961]{0,1:T(8,128)} fusion(f32[3,8961]{0,1:T(8,128)} %scatter_custom_fusion.7, s32[2048]{0:T(1024)S(1)} %bitcast.289, f32[3,2048]{0,1:T(8,128)S(1)} %bitcast_multiply_fusion), kind=kCustom, calls=%fused_computation.34 | custom fusion | flops 6144 | bytes 1156108 | tf_op jit(solution)/shard_map/scatter-add | solution.py:67
  557.0 5.4 collective-permute-start.24
  562.4 4.4 collective-permute-start.25
  576.6 4.9 collective-permute-start.30
  581.6 5.4 collective-permute-start.31
  592.0 14.1 %scatter_fusion.3 = f32[3,6912]{0,1:T(8,128)} fusion(f32[3,6912]{0,1:T(8,128)} %slice.299, s32[2048]{0:T(1024)S(1)} %bitcast.275, f32[2048,3]{1,0:T(8,128)S(1)} %bitcast.246), kind=kCustom, calls=%fused_computation.22 | custom fusion | flops 6144 | bytes 81920 | tf_op jit(solution)/shard_map/scatter-add | solution.py:131
  611.3 7.5 gather_fusion.8
  621.1 5.0 collective-permute-start.33
  629.9 7.6 collective-permute-start.36
  655.0 7.8 gather_fusion.9
  663.1 5.2 scatter_fusion.4
  668.3 7.8 fusion.24
  676.1 56.8 %gather_fusion.11 = f32[16384,3]{1,0:T(8,128)} fusion(f32[3,8960]{0,1:T(8,128)} %get-tuple-element.15, s32[16384]{0:T(1024)S(1)} %broadcast_clamp_fusion), kind=kCustom, calls=%fused_computation.11 | custom fusion | bytes 458752 | tf_op jit(solution)/shard_map/gather | solution.py:138
  732.9 5.2 copy.295
  738.1 56.8 %gather_fusion.10 = f32[16384,3]{1,0:T(8,128)} fusion(f32[3,8960]{0,1:T(8,128)} %get-tuple-element.14, s32[16384]{0:T(1024)S(1)} %broadcast_clamp_fusion), kind=kCustom, calls=%fused_computation.10 | custom fusion | bytes 458752 | tf_op jit(solution)/shard_map/gather | solution.py:137
  794.9 5.3 copy.294
  800.7 6.2 gather_fusion.12
  816.7 6.7 collective-permute-start.44
  830.2 6.1 collective-permute-start.47
  837.6 7.6 scatter_custom_fusion.11
  (225 shorter events, 153.9 us)
Async XLA Ops:
  12.5 20.4 %collective-permute-start = (f32[3,256]{1,0:T(4,128)S(1)}, f32[3,256]{1,0:T(4,128)S(1)}, u32[]{:S(2)}, u32[]{:S(2)}) collective-permute-start(f32[3,256]{1,0:T(4,128)S(1)} %get-tuple-element.57), channel_id=1, source_target_pairs={{0,1},{1,2},{2,3},{3,4},{4,5},{5,6},{6,7},{7,8},{8,9},{9,10},{10,1... | collective-permute-start | bytes 9224 | tf_op jit(solution)/shard_map/ppermute | solution.py:20
  14.4 21.0 %collective-permute-start.1 = (f32[3,256]{1,0:T(4,128)S(1)}, f32[3,256]{1,0:T(4,128)S(1)}, u32[]{:S(2)}, u32[]{:S(2)}) collective-permute-start(f32[3,256]{1,0:T(4,128)S(1)} %get-tuple-element.56), channel_id=1, source_target_pairs={{0,2},{1,3},{2,4},{3,5},{4,6},{5,7},{6,8},{7,9},{8,10},{9,11},{10,... | collective-permute-start | bytes 9224 | tf_op jit(solution)/shard_map/ppermute | solution.py:20
  17.9 19.9 %collective-permute-start.2 = (f32[3,256]{1,0:T(4,128)S(1)}, f32[3,256]{1,0:T(4,128)S(1)}, u32[]{:S(2)}, u32[]{:S(2)}) collective-permute-start(f32[3,256]{1,0:T(4,128)S(1)} %get-tuple-element.55), channel_id=1, source_target_pairs={{0,3},{1,4},{2,5},{3,6},{4,7},{5,8},{6,9},{7,10},{8,11},{9,12},{10... | collective-permute-start | bytes 9224 | tf_op jit(solution)/shard_map/ppermute | solution.py:20
  22.1 20.9 %collective-permute-start.3 = (f32[3,256]{1,0:T(4,128)S(1)}, f32[3,256]{1,0:T(4,128)S(1)}, u32[]{:S(2)}, u32[]{:S(2)}) collective-permute-start(f32[3,256]{1,0:T(4,128)S(1)} %get-tuple-element.54), channel_id=1, source_target_pairs={{0,4},{1,5},{2,6},{3,7},{4,8},{5,9},{6,10},{7,11},{8,12},{9,13},{1... | collective-permute-start | bytes 9224 | tf_op jit(solution)/shard_map/ppermute | solution.py:20
  27.2 15.8 %collective-permute-start.4 = (f32[3,256]{1,0:T(4,128)S(1)}, f32[3,256]{1,0:T(4,128)S(1)}, u32[]{:S(2)}, u32[]{:S(2)}) collective-permute-start(f32[3,256]{1,0:T(4,128)S(1)} %get-tuple-element.53), channel_id=1, source_target_pairs={{1,0},{2,1},{3,2},{4,3},{5,4},{6,5},{7,6},{8,7},{9,8},{10,9},{11,1... | collective-permute-start | bytes 9224 | tf_op jit(solution)/shard_map/ppermute | solution.py:20
  32.9 10.1 %collective-permute-start.5 = (f32[3,256]{1,0:T(4,128)S(1)}, f32[3,256]{1,0:T(4,128)S(1)}, u32[]{:S(2)}, u32[]{:S(2)}) collective-permute-start(f32[3,256]{1,0:T(4,128)S(1)} %get-tuple-element.52), channel_id=1, source_target_pairs={{2,0},{3,1},{4,2},{5,3},{6,4},{7,5},{8,6},{9,7},{10,8},{11,9},{12,... | collective-permute-start | bytes 9224 | tf_op jit(solution)/shard_map/ppermute | solution.py:20
  35.4 7.7 collective-permute-start.6
  37.8 7.0 collective-permute-start.7
  257.2 17.4 %collective-permute-start.8 = (f32[3,256]{1,0:T(4,128)S(1)}, f32[3,256]{1,0:T(4,128)S(1)}, u32[]{:S(2)}, u32[]{:S(2)}) collective-permute-start(f32[3,256]{1,0:T(4,128)S(1)} %get-tuple-element.49), channel_id=1, source_target_pairs={{1,0},{2,1},{3,2},{4,3},{5,4},{6,5},{7,6},{8,7},{9,8},{10,9},{11,1... | collective-permute-start | bytes 9224 | tf_op jit(solution)/shard_map/ppermute | solution.py:20
  261.7 14.9 %collective-permute-start.9 = (f32[3,256]{1,0:T(4,128)S(1)}, f32[3,256]{1,0:T(4,128)S(1)}, u32[]{:S(2)}, u32[]{:S(2)}) collective-permute-start(f32[3,256]{1,0:T(4,128)S(1)} %get-tuple-element.48), channel_id=1, source_target_pairs={{2,0},{3,1},{4,2},{5,3},{6,4},{7,5},{8,6},{9,7},{10,8},{11,9},{12,... | collective-permute-start | bytes 9224 | tf_op jit(solution)/shard_map/ppermute | solution.py:20
  266.5 15.1 %collective-permute-start.10 = (f32[3,256]{1,0:T(4,128)S(1)}, f32[3,256]{1,0:T(4,128)S(1)}, u32[]{:S(2)}, u32[]{:S(2)}) collective-permute-start(f32[3,256]{1,0:T(4,128)S(1)} %get-tuple-element.47), channel_id=1, source_target_pairs={{3,0},{4,1},{5,2},{6,3},{7,4},{8,5},{9,6},{10,7},{11,8},{12,9},{13... | collective-permute-start | bytes 9224 | tf_op jit(solution)/shard_map/ppermute | solution.py:20
  269.3 20.7 %collective-permute-start.11 = (f32[3,256]{1,0:T(4,128)S(1)}, f32[3,256]{1,0:T(4,128)S(1)}, u32[]{:S(2)}, u32[]{:S(2)}) collective-permute-start(f32[3,256]{1,0:T(4,128)S(1)} %get-tuple-element.46), channel_id=1, source_target_pairs={{4,0},{5,1},{6,2},{7,3},{8,4},{9,5},{10,6},{11,7},{12,8},{13,9},{1... | collective-permute-start | bytes 9224 | tf_op jit(solution)/shard_map/ppermute | solution.py:20
  272.4 17.7 %collective-permute-start.12 = (f32[3,256]{1,0:T(4,128)S(1)}, f32[3,256]{1,0:T(4,128)S(1)}, u32[]{:S(2)}, u32[]{:S(2)}) collective-permute-start(f32[3,256]{1,0:T(4,128)S(1)} %get-tuple-element.45), channel_id=1, source_target_pairs={{0,1},{1,2},{2,3},{3,4},{4,5},{5,6},{6,7},{7,8},{8,9},{9,10},{10,1... | collective-permute-start | bytes 9224 | tf_op jit(solution)/shard_map/ppermute | solution.py:20
  274.5 15.6 %collective-permute-start.13 = (f32[3,256]{1,0:T(4,128)S(1)}, f32[3,256]{1,0:T(4,128)S(1)}, u32[]{:S(2)}, u32[]{:S(2)}) collective-permute-start(f32[3,256]{1,0:T(4,128)S(1)} %get-tuple-element.44), channel_id=1, source_target_pairs={{0,2},{1,3},{2,4},{3,5},{4,6},{5,7},{6,8},{7,9},{8,10},{9,11},{10,... | collective-permute-start | bytes 9224 | tf_op jit(solution)/shard_map/ppermute | solution.py:20
  276.6 13.5 %collective-permute-start.14 = (f32[3,256]{1,0:T(4,128)S(1)}, f32[3,256]{1,0:T(4,128)S(1)}, u32[]{:S(2)}, u32[]{:S(2)}) collective-permute-start(f32[3,256]{1,0:T(4,128)S(1)} %get-tuple-element.43), channel_id=1, source_target_pairs={{0,3},{1,4},{2,5},{3,6},{4,7},{5,8},{6,9},{7,10},{8,11},{9,12},{10... | collective-permute-start | bytes 9224 | tf_op jit(solution)/shard_map/ppermute | solution.py:20
  281.7 10.0 %collective-permute-start.15 = (f32[3,256]{1,0:T(4,128)S(1)}, f32[3,256]{1,0:T(4,128)S(1)}, u32[]{:S(2)}, u32[]{:S(2)}) collective-permute-start(f32[3,256]{1,0:T(4,128)S(1)} %get-tuple-element.42), channel_id=1, source_target_pairs={{0,4},{1,5},{2,6},{3,7},{4,8},{5,9},{6,10},{7,11},{8,12},{9,13},{1... | collective-permute-start | bytes 9224 | tf_op jit(solution)/shard_map/ppermute | solution.py:20
  319.0 17.3 %collective-permute-start.16 = (f32[3,256]{1,0:T(4,128)S(1)}, f32[3,256]{1,0:T(4,128)S(1)}, u32[]{:S(2)}, u32[]{:S(2)}) collective-permute-start(f32[3,256]{1,0:T(4,128)S(1)} %get-tuple-element.41), channel_id=1, source_target_pairs={{0,1},{1,2},{2,3},{3,4},{4,5},{5,6},{6,7},{7,8},{8,9},{9,10},{10,1... | collective-permute-start | bytes 9224 | tf_op jit(solution)/shard_map/ppermute | solution.py:20
  321.0 18.4 %collective-permute-start.17 = (f32[3,256]{1,0:T(4,128)S(1)}, f32[3,256]{1,0:T(4,128)S(1)}, u32[]{:S(2)}, u32[]{:S(2)}) collective-permute-start(f32[3,256]{1,0:T(4,128)S(1)} %get-tuple-element.40), channel_id=1, source_target_pairs={{0,2},{1,3},{2,4},{3,5},{4,6},{5,7},{6,8},{7,9},{8,10},{9,11},{10,... | collective-permute-start | bytes 9224 | tf_op jit(solution)/shard_map/ppermute | solution.py:20
  324.9 18.3 %collective-permute-start.18 = (f32[3,256]{1,0:T(4,128)S(1)}, f32[3,256]{1,0:T(4,128)S(1)}, u32[]{:S(2)}, u32[]{:S(2)}) collective-permute-start(f32[3,256]{1,0:T(4,128)S(1)} %get-tuple-element.39), channel_id=1, source_target_pairs={{0,3},{1,4},{2,5},{3,6},{4,7},{5,8},{6,9},{7,10},{8,11},{9,12},{10... | collective-permute-start | bytes 9224 | tf_op jit(solution)/shard_map/ppermute | solution.py:20
  326.8 21.7 %collective-permute-start.19 = (f32[3,256]{1,0:T(4,128)S(1)}, f32[3,256]{1,0:T(4,128)S(1)}, u32[]{:S(2)}, u32[]{:S(2)}) collective-permute-start(f32[3,256]{1,0:T(4,128)S(1)} %get-tuple-element.38), channel_id=1, source_target_pairs={{0,4},{1,5},{2,6},{3,7},{4,8},{5,9},{6,10},{7,11},{8,12},{9,13},{1... | collective-permute-start | bytes 9224 | tf_op jit(solution)/shard_map/ppermute | solution.py:20
  328.7 19.8 %collective-permute-start.20 = (f32[3,256]{1,0:T(4,128)S(1)}, f32[3,256]{1,0:T(4,128)S(1)}, u32[]{:S(2)}, u32[]{:S(2)}) collective-permute-start(f32[3,256]{1,0:T(4,128)S(1)} %get-tuple-element.37), channel_id=1, source_target_pairs={{1,0},{2,1},{3,2},{4,3},{5,4},{6,5},{7,6},{8,7},{9,8},{10,9},{11,1... | collective-permute-start | bytes 9224 | tf_op jit(solution)/shard_map/ppermute | solution.py:20
  336.3 12.2 %collective-permute-start.21 = (f32[3,256]{1,0:T(4,128)S(1)}, f32[3,256]{1,0:T(4,128)S(1)}, u32[]{:S(2)}, u32[]{:S(2)}) collective-permute-start(f32[3,256]{1,0:T(4,128)S(1)} %get-tuple-element.36), channel_id=1, source_target_pairs={{2,0},{3,1},{4,2},{5,3},{6,4},{7,5},{8,6},{9,7},{10,8},{11,9},{12,... | collective-permute-start | bytes 9224 | tf_op jit(solution)/shard_map/ppermute | solution.py:20
  339.4 9.2 %collective-permute-start.22 = (f32[3,256]{1,0:T(4,128)S(1)}, f32[3,256]{1,0:T(4,128)S(1)}, u32[]{:S(2)}, u32[]{:S(2)}) collective-permute-start(f32[3,256]{1,0:T(4,128)S(1)} %get-tuple-element.35), channel_id=1, source_target_pairs={{3,0},{4,1},{5,2},{6,3},{7,4},{8,5},{9,6},{10,7},{11,8},{12,9},{13... | collective-permute-start | bytes 9224 | tf_op jit(solution)/shard_map/ppermute | solution.py:20
  343.2 7.0 collective-permute-start.23
  557.0 16.7 %collective-permute-start.24 = (f32[3,256]{1,0:T(4,128)S(1)}, f32[3,256]{1,0:T(4,128)S(1)}, u32[]{:S(2)}, u32[]{:S(2)}) collective-permute-start(f32[3,256]{1,0:T(4,128)S(1)} %get-tuple-element.33), channel_id=1, source_target_pairs={{1,0},{2,1},{3,2},{4,3},{5,4},{6,5},{7,6},{8,7},{9,8},{10,9},{11,1... | collective-permute-start | bytes 9224 | tf_op jit(solution)/shard_map/ppermute | solution.py:20
  562.4 14.3 %collective-permute-start.25 = (f32[3,256]{1,0:T(4,128)S(1)}, f32[3,256]{1,0:T(4,128)S(1)}, u32[]{:S(2)}, u32[]{:S(2)}) collective-permute-start(f32[3,256]{1,0:T(4,128)S(1)} %get-tuple-element.32), channel_id=1, source_target_pairs={{2,0},{3,1},{4,2},{5,3},{6,4},{7,5},{8,6},{9,7},{10,8},{11,9},{12,... | collective-permute-start | bytes 9224 | tf_op jit(solution)/shard_map/ppermute | solution.py:20
  566.8 14.8 %collective-permute-start.26 = (f32[3,256]{1,0:T(4,128)S(1)}, f32[3,256]{1,0:T(4,128)S(1)}, u32[]{:S(2)}, u32[]{:S(2)}) collective-permute-start(f32[3,256]{1,0:T(4,128)S(1)} %get-tuple-element.31), channel_id=1, source_target_pairs={{3,0},{4,1},{5,2},{6,3},{7,4},{8,5},{9,6},{10,7},{11,8},{12,9},{13... | collective-permute-start | bytes 9224 | tf_op jit(solution)/shard_map/ppermute | solution.py:20
  569.2 21.9 %collective-permute-start.27 = (f32[3,256]{1,0:T(4,128)S(1)}, f32[3,256]{1,0:T(4,128)S(1)}, u32[]{:S(2)}, u32[]{:S(2)}) collective-permute-start(f32[3,256]{1,0:T(4,128)S(1)} %get-tuple-element.30), channel_id=1, source_target_pairs={{4,0},{5,1},{6,2},{7,3},{8,4},{9,5},{10,6},{11,7},{12,8},{13,9},{1... | collective-permute-start | bytes 9224 | tf_op jit(solution)/shard_map/ppermute | solution.py:20
  571.2 20.0 %collective-permute-start.28 = (f32[3,256]{1,0:T(4,128)S(1)}, f32[3,256]{1,0:T(4,128)S(1)}, u32[]{:S(2)}, u32[]{:S(2)}) collective-permute-start(f32[3,256]{1,0:T(4,128)S(1)} %get-tuple-element.29), channel_id=1, source_target_pairs={{0,1},{1,2},{2,3},{3,4},{4,5},{5,6},{6,7},{7,8},{8,9},{9,10},{10,1... | collective-permute-start | bytes 9224 | tf_op jit(solution)/shard_map/ppermute | solution.py:20
  573.6 17.5 %collective-permute-start.29 = (f32[3,256]{1,0:T(4,128)S(1)}, f32[3,256]{1,0:T(4,128)S(1)}, u32[]{:S(2)}, u32[]{:S(2)}) collective-permute-start(f32[3,256]{1,0:T(4,128)S(1)} %get-tuple-element.28), channel_id=1, source_target_pairs={{0,2},{1,3},{2,4},{3,5},{4,6},{5,7},{6,8},{7,9},{8,10},{9,11},{10,... | collective-permute-start | bytes 9224 | tf_op jit(solution)/shard_map/ppermute | solution.py:20
  576.6 14.5 %collective-permute-start.30 = (f32[3,256]{1,0:T(4,128)S(1)}, f32[3,256]{1,0:T(4,128)S(1)}, u32[]{:S(2)}, u32[]{:S(2)}) collective-permute-start(f32[3,256]{1,0:T(4,128)S(1)} %get-tuple-element.27), channel_id=1, source_target_pairs={{0,3},{1,4},{2,5},{3,6},{4,7},{5,8},{6,9},{7,10},{8,11},{9,12},{10... | collective-permute-start | bytes 9224 | tf_op jit(solution)/shard_map/ppermute | solution.py:20
  581.6 10.0 %collective-permute-start.31 = (f32[3,256]{1,0:T(4,128)S(1)}, f32[3,256]{1,0:T(4,128)S(1)}, u32[]{:S(2)}, u32[]{:S(2)}) collective-permute-start(f32[3,256]{1,0:T(4,128)S(1)} %get-tuple-element.26), channel_id=1, source_target_pairs={{0,4},{1,5},{2,6},{3,7},{4,8},{5,9},{6,10},{7,11},{8,12},{9,13},{1... | collective-permute-start | bytes 9224 | tf_op jit(solution)/shard_map/ppermute | solution.py:20
  619.1 18.5 %collective-permute-start.32 = (f32[6,256]{1,0:T(8,128)S(1)}, f32[6,256]{1,0:T(8,128)S(1)}, u32[]{:S(2)}, u32[]{:S(2)}) collective-permute-start(f32[6,256]{1,0:T(8,128)S(1)} %get-tuple-element.25), channel_id=1, source_target_pairs={{0,1},{1,2},{2,3},{3,4},{4,5},{5,6},{6,7},{7,8},{8,9},{9,10},{10,1... | collective-permute-start | bytes 18440 | tf_op jit(solution)/shard_map/ppermute | solution.py:20
  621.1 19.5 %collective-permute-start.33 = (f32[6,256]{1,0:T(8,128)S(1)}, f32[6,256]{1,0:T(8,128)S(1)}, u32[]{:S(2)}, u32[]{:S(2)}) collective-permute-start(f32[6,256]{1,0:T(8,128)S(1)} %get-tuple-element.24), channel_id=1, source_target_pairs={{0,2},{1,3},{2,4},{3,5},{4,6},{5,7},{6,8},{7,9},{8,10},{9,11},{10,... | collective-permute-start | bytes 18440 | tf_op jit(solution)/shard_map/ppermute | solution.py:20
  626.1 18.4 %collective-permute-start.34 = (f32[6,256]{1,0:T(8,128)S(1)}, f32[6,256]{1,0:T(8,128)S(1)}, u32[]{:S(2)}, u32[]{:S(2)}) collective-permute-start(f32[6,256]{1,0:T(8,128)S(1)} %get-tuple-element.23), channel_id=1, source_target_pairs={{0,3},{1,4},{2,5},{3,6},{4,7},{5,8},{6,9},{7,10},{8,11},{9,12},{10... | collective-permute-start | bytes 18440 | tf_op jit(solution)/shard_map/ppermute | solution.py:20
  628.0 20.6 %collective-permute-start.35 = (f32[6,256]{1,0:T(8,128)S(1)}, f32[6,256]{1,0:T(8,128)S(1)}, u32[]{:S(2)}, u32[]{:S(2)}) collective-permute-start(f32[6,256]{1,0:T(8,128)S(1)} %get-tuple-element.22), channel_id=1, source_target_pairs={{0,4},{1,5},{2,6},{3,7},{4,8},{5,9},{6,10},{7,11},{8,12},{9,13},{1... | collective-permute-start | bytes 18440 | tf_op jit(solution)/shard_map/ppermute | solution.py:20
  629.9 18.7 %collective-permute-start.36 = (f32[6,256]{1,0:T(8,128)S(1)}, f32[6,256]{1,0:T(8,128)S(1)}, u32[]{:S(2)}, u32[]{:S(2)}) collective-permute-start(f32[6,256]{1,0:T(8,128)S(1)} %get-tuple-element.21), channel_id=1, source_target_pairs={{1,0},{2,1},{3,2},{4,3},{5,4},{6,5},{7,6},{8,7},{9,8},{10,9},{11,1... | collective-permute-start | bytes 18440 | tf_op jit(solution)/shard_map/ppermute | solution.py:20
  637.5 11.1 %collective-permute-start.37 = (f32[6,256]{1,0:T(8,128)S(1)}, f32[6,256]{1,0:T(8,128)S(1)}, u32[]{:S(2)}, u32[]{:S(2)}) collective-permute-start(f32[6,256]{1,0:T(8,128)S(1)} %get-tuple-element.20), channel_id=1, source_target_pairs={{2,0},{3,1},{4,2},{5,3},{6,4},{7,5},{8,6},{9,7},{10,8},{11,9},{12,... | collective-permute-start | bytes 18440 | tf_op jit(solution)/shard_map/ppermute | solution.py:20
  640.6 8.1 collective-permute-start.38
  644.4 7.0 collective-permute-start.39
  806.9 16.5 %collective-permute-start.40 = (f32[128]{0:T(128)S(1)}, f32[128]{0:T(128)S(1)}, u32[]{:S(2)}, u32[]{:S(2)}) collective-permute-start(f32[128]{0:T(128)S(1)} %get-tuple-element.67), channel_id=1, source_target_pairs={{0,1},{1,2},{2,3},{3,4},{4,5},{5,6},{6,7},{7,8},{8,9},{9,10},{10,1... | collective-permute-start | bytes 1544 | tf_op jit(solution)/shard_map/ppermute | solution.py:20
  808.8 17.7 %collective-permute-start.41 = (f32[128]{0:T(128)S(1)}, f32[128]{0:T(128)S(1)}, u32[]{:S(2)}, u32[]{:S(2)}) collective-permute-start(f32[128]{0:T(128)S(1)} %get-tuple-element.66), channel_id=1, source_target_pairs={{0,2},{1,3},{2,4},{3,5},{4,6},{5,7},{6,8},{7,9},{8,10},{9,11},{10,... | collective-permute-start | bytes 1544 | tf_op jit(solution)/shard_map/ppermute | solution.py:20
  810.7 19.5 %collective-permute-start.42 = (f32[128]{0:T(128)S(1)}, f32[128]{0:T(128)S(1)}, u32[]{:S(2)}, u32[]{:S(2)}) collective-permute-start(f32[128]{0:T(128)S(1)} %get-tuple-element.65), channel_id=1, source_target_pairs={{0,3},{1,4},{2,5},{3,6},{4,7},{5,8},{6,9},{7,10},{8,11},{9,12},{10... | collective-permute-start | bytes 1544 | tf_op jit(solution)/shard_map/ppermute | solution.py:20
  813.8 22.5 %collective-permute-start.43 = (f32[128]{0:T(128)S(1)}, f32[128]{0:T(128)S(1)}, u32[]{:S(2)}, u32[]{:S(2)}) collective-permute-start(f32[128]{0:T(128)S(1)} %get-tuple-element.64), channel_id=1, source_target_pairs={{0,4},{1,5},{2,6},{3,7},{4,8},{5,9},{6,10},{7,11},{8,12},{9,13},{1... | collective-permute-start | bytes 1544 | tf_op jit(solution)/shard_map/ppermute | solution.py:20
  816.7 19.7 %collective-permute-start.44 = (f32[128]{0:T(128)S(1)}, f32[128]{0:T(128)S(1)}, u32[]{:S(2)}, u32[]{:S(2)}) collective-permute-start(f32[128]{0:T(128)S(1)} %get-tuple-element.63), channel_id=1, source_target_pairs={{1,0},{2,1},{3,2},{4,3},{5,4},{6,5},{7,6},{8,7},{9,8},{10,9},{11,1... | collective-permute-start | bytes 1544 | tf_op jit(solution)/shard_map/ppermute | solution.py:20
  823.4 12.9 %collective-permute-start.45 = (f32[128]{0:T(128)S(1)}, f32[128]{0:T(128)S(1)}, u32[]{:S(2)}, u32[]{:S(2)}) collective-permute-start(f32[128]{0:T(128)S(1)} %get-tuple-element.62), channel_id=1, source_target_pairs={{2,0},{3,1},{4,2},{5,3},{6,4},{7,5},{8,6},{9,7},{10,8},{11,9},{12,... | collective-permute-start | bytes 1544 | tf_op jit(solution)/shard_map/ppermute | solution.py:20
  826.5 9.9 %collective-permute-start.46 = (f32[128]{0:T(128)S(1)}, f32[128]{0:T(128)S(1)}, u32[]{:S(2)}, u32[]{:S(2)}) collective-permute-start(f32[128]{0:T(128)S(1)} %get-tuple-element.61), channel_id=1, source_target_pairs={{3,0},{4,1},{5,2},{6,3},{7,4},{8,5},{9,6},{10,7},{11,8},{12,9},{13... | collective-permute-start | bytes 1544 | tf_op jit(solution)/shard_map/ppermute | solution.py:20
  830.2 7.3 collective-permute-start.47
  (15 other events, 481.3 us)
where the time goes:
time: 848 us; the launch traced here: 846 us
  local copies, waits for them, and re-layouts  399 us (47%)
  other arithmetic  257 us (30%)
  starting transfers between devices  177 us (21%)
  waiting for transfers between devices  9.4 us (1%)
    scatter-add x2, other arithmetic, local_product(): jnp.zeros_like(fixed).at[:, connect]  180 us
    ppermute x48, starting transfers between devices, from_behind(): return lax.ppermute(block, axis, route)  177 us
    gather x4, local copies, waits for them, and re-layouts, local_product(): cells = fixed[:, connect].reshape(3 * connect.shape[0], -1)  124 us
    gather x2, local copies, waits for them, and re-layouts, local(): adjoint_cells = fixed[:3][:, connect].reshape(3 * connect.shape[0], -1)  62.1 us
    gather x2, local copies, waits for them, and re-layouts, local(): primal_cells = fixed[3:][:, connect].reshape(3 * connect.shape[0], -1)  62 us
    scatter-add x2, other arithmetic, release(): padded.at[:, master.reshape(-1)].add(spread.reshape(totals.shape[0], -1))  29.5 us
    scatter-add x2, other arithmetic, local(): owned_part.at[:, export_rows.reshape(-1)]  28.2 us
    gather x6, local copies, waits for them, and re-layouts, extend(): blocks = jnp.moveaxis(owned[:, export_rows], 1, 0)  23.4 us
  transfers between devices with their start and end apart: 48, of which 6 were waited for; matrix products, arithmetic and copies ran while one was open for 1% of the time, Pallas kernels for 0%

commit v1 on v0

v1 whole, which is shorter than its diff:
```python
import jax
import jax.numpy as jnp
from jax import lax
from jax.experimental import pallas as pl
from jax.experimental.pallas import tpu as pltpu
from jax.sharding import PartitionSpec as P

MESH = pl.DeviceIdType.MESH
F32 = jnp.float32
BF16 = jnp.bfloat16

REACH = 4
SLOTS = 2 * REACH
SWEEPS = 2
NODES_DEV = 6912
EXT = 8960
PAD_CODE = 16368
RELAXATION = 0.7

LANES = 256
OWNED = 27
GHOST_ROW = 32
ROWS = 40
OFFSETS = [step + 1 for step in range(REACH)] + [-(step + 1) for step in range(REACH)]


def modulo(values, divisor):
    quotient = ((values.astype(F32) + 0.5) * (1.0 / divisor)).astype(jnp.int32)
    return values - quotient * divisor


def place(slots):
    row = slots >> 8
    return row + jnp.where(row >= OWNED, GHOST_ROW - OWNED, 0), slots & 255


def one_hot(row, count, dtype):
    spots = lax.broadcasted_iota(jnp.int32, (count, row.shape[1]), 0)
    return jnp.where(spots == row, 1.0, 0.0).astype(dtype)


def halves(values):
    high = values.astype(BF16).astype(F32)
    return jnp.concatenate([high, values - high], 0).astype(BF16)


def dot(a, b):
    return jnp.dot(a, b, preferred_element_type=F32)


def dot_nt(a, b):
    return lax.dot_general(a, b, (((1,), (1,)), ((), ())), preferred_element_type=F32)


def dot_tn(a, b):
    return lax.dot_general(a, b, (((0,), (0,)), ((), ())), preferred_element_type=F32)


def joined(values):
    half = values.shape[0] // 2
    return values[:half] + values[half:]


def picked(table, lane_hot, row_hot, parts, rows):
    found = joined(dot(table, lane_hot))
    return [
        jnp.sum(found[part * rows : (part + 1) * rows] * row_hot, axis=0, keepdims=True)
        for part in range(parts)
    ]


def spread(values, row_hot):
    return halves(jnp.concatenate([row_hot * value for value in values], 0))


def kernel(
    start_ref,
    source_ref,
    inverse_ref,
    primal_ref,
    load_ref,
    modulus_ref,
    stiff_ref,
    connect_ref,
    node_ref,
    master_ref,
    weight_ref,
    lists_ref,
    sub_cell_ref,
    sub_face_ref,
    sub_owner_ref,
    adjoint_ref,
    indicator_ref,
    table,
    primal_table,
    source,
    inverse,
    row_hots,
    lane_hots,
    list_rows,
    list_lanes,
    master_rows,
    master_lanes,
    node_rows,
    node_lanes,
    keep,
    sub_rows,
    sub_lanes,
    owner_lanes,
    cells,
    image,
    primal_cells,
    send_first,
    recv_first,
    send_ghost,
    recv_ghost,
    send_sub,
    recv_sub,
    send_sem,
    recv_sem,
):
    me = lax.axis_index("dom")
    count = lax.axis_size("dom")

    def device(offset):
        return lax.rem(me + offset + count, count)

    barrier = pltpu.get_barrier_semaphore()
    for offset in OFFSETS:
        pl.semaphore_signal(barrier, inc=1, device_id=(device(offset),), device_id_type=MESH)

    def exchange(send, recv, turn, direction):
        copies = []
        for slot, offset in enumerate(OFFSETS):
            copies.append(
                pltpu.make_async_remote_copy(
                    src_ref=send.at[slot],
                    dst_ref=recv.at[slot],
                    send_sem=send_sem.at[turn, slot],
                    recv_sem=recv_sem.at[turn, slot],
                    device_id=(device(direction * offset),),
                    device_id_type=MESH,
                )
            )
        for copy in copies:
            copy.start()
        return copies

    def arrived(slot, direction, values):
        origin = me - direction * OFFSETS[slot]
        inside = jnp.logical_and(origin >= 0, origin < count)
        return jnp.where(inside, values, 0.0)

    table[...] = jnp.zeros_like(table)
    primal_table[...] = jnp.zeros_like(primal_table)
    source[...] = jnp.zeros_like(source)
    inverse[...] = jnp.zeros_like(inverse)
    for part in range(3):
        for row in range(OWNED):
            spot = pl.ds(row * LANES, LANES)
            table[part * ROWS + row, :] = start_ref[part, spot]
            primal_table[part * ROWS + row, :] = primal_ref[part, spot]
            source[part * GHOST_ROW + row, :] = source_ref[part, spot]
            inverse[part * GHOST_ROW + row, :] = inverse_ref[part, spot]

    lane_ids = lax.broadcasted_iota(jnp.int32, (SLOTS, LANES), 1)
    lists = modulo(17 * lists_ref[...] + lane_ids, NODES_DEV)
    for slot in range(SLOTS):
        row = lists[slot : slot + 1]
        spot = pl.ds(slot * LANES, LANES)
        list_lanes[:, spot] = one_hot(row & 255, LANES, BF16)
        list_rows[:, spot] = one_hot(row >> 8, GHOST_ROW, F32)

    def owned_of(ref):
        return jnp.concatenate(
            [ref[pl.ds(part * ROWS, GHOST_ROW), :] for part in range(3)], 0
        )

    def export(values, send, parts):
        stacked = halves(values)
        for slot in range(SLOTS):
            spot = pl.ds(slot * LANES, LANES)
            rows = picked(stacked, list_lanes[:, spot], list_rows[:, spot], parts, GHOST_ROW)
            for part in range(parts):
                send[slot, 2 * part : 2 * part + 1, :] = rows[part][:, :128]
                send[slot, 2 * part + 1 : 2 * part + 2, :] = rows[part][:, 128:]

    def import_into(ref, recv, first):
        for slot in range(SLOTS):
            block = arrived(slot, 1, recv[slot])
            for part in range(3):
                spot = 2 * (first + part)
                ref[pl.ds(part * ROWS + GHOST_ROW + slot, 1), pl.ds(0, 128)] = block[
                    spot : spot + 1
                ]
                ref[pl.ds(part * ROWS + GHOST_ROW + slot, 1), pl.ds(128, 128)] = block[
                    spot + 1 : spot + 2
                ]

    export(jnp.concatenate([owned_of(table), owned_of(primal_table)], 0), send_first, 6)
    pl.semaphore_wait(barrier, SLOTS)
    pending = exchange(send_first, recv_first, 0, 1)

    def build(block, carry):
        rows = connect_ref[pl.ds(pl.multiple_of(block * 8, 8), 8), :]
        row_ids, lanes = place(modulo(17 * rows + 27 * lane_ids, EXT))
        for step in range(8):
            spot = pl.ds(step * LANES, LANES)
            lane_hots[block, :, spot] = one_hot(lanes[step : step + 1], LANES, BF16)
            row_hots[block, :, spot] = one_hot(row_ids[step : step + 1], ROWS, F32)
        return carry

    lax.fori_loop(0, 8, build, 0)

    hang_ids = lax.broadcasted_iota(jnp.int32, (16, 128), 1)
    row_ids, lanes = place(modulo(17 * master_ref[...] + 8 * hang_ids, EXT))
    weight = weight_ref[...]
    for step in range(16):
        spot = pl.ds(step * 128, 128)
        master_lanes[:, spot] = one_hot(lanes[step : step + 1], LANES, BF16)
        master_rows[:, spot] = (
            one_hot(row_ids[step : step + 1], ROWS, F32) * weight[step : step + 1]
        )
    node = node_ref[...]
    spots = modulo(13 * node, NODES_DEV)
    hang_row = jnp.where(node == PAD_CODE, -1, spots >> 8)
    node_lanes[...] = one_hot(spots & 255, LANES, BF16)
    node_rows[...] = one_hot(hang_row, ROWS, F32)
    keep[...] = 1.0 - dot_nt(one_hot(hang_row, 48, BF16), node_lanes[...])[:ROWS]
    for slot in range(SLOTS):
        spot = pl.ds(slot * 128, 128)
        sub_lanes[:, spot] = one_hot(sub_cell_ref[slot : slot + 1, :], LANES, BF16)
        sub_rows[:, spot] = one_hot(sub_face_ref[slot : slot + 1, :], 8, F32)
        owner_lanes[:, spot] = one_hot(sub_owner_ref[slot : slot + 1, :], LANES, BF16)

    stiff = stiff_ref[...]
    stiff_high = stiff.astype(BF16)
    stiff_low = (stiff - stiff_high.astype(F32)).astype(BF16)
    modulus = modulus_ref[...]

    def kept(values):
        return jnp.concatenate(
            [values[part * ROWS : (part + 1) * ROWS] * keep[...] for part in range(3)], 0
        )

    def constrain(values):
        stacked = halves(values)
        totals = [jnp.zeros((8, LANES), F32)] * 3
        for step in range(8):
            spot = pl.ds(step * LANES, LANES)
            found = joined(dot(stacked, master_lanes[:, spot]))
            for part in range(3):
                term = found[part * ROWS : (part + 1) * ROWS] * master_rows[:, spot]
                for group in range(ROWS // 8):
                    totals[part] = totals[part] + term[group * 8 : group * 8 + 8]
        sums = [jnp.sum(total, axis=0, keepdims=True) for total in totals]
        sums = [each[:, :128] + each[:, 128:] for each in sums]
        written = joined(dot_nt(spread(sums, node_rows[...]), node_lanes[...]))
        return kept(values) + written

    def gather_cells(values, out):
        stacked = halves(values)

        def body(block, carry):
            found = [[], [], []]
            for step in range(8):
                spot = pl.ds(step * LANES, LANES)
                rows = picked(
                    stacked, lane_hots[block, :, spot], row_hots[block, :, spot], 3, ROWS
                )
                for part in range(3):
                    found[part].append(rows[part])
            for part in range(3):
                spot = pl.ds(pl.multiple_of(part * 64 + block * 8, 8), 8)
                out[spot, :] = jnp.concatenate(found[part], 0)
            return carry

        lax.fori_loop(0, 8, body, 0)

    def scatter_cells(values):
        def body(block, total):
            columns = []
            rows = [
                values[pl.ds(pl.multiple_of(part * 64 + block * 8, 8), 8), :] for part in range(3)
            ]
            for step in range(8):
                spot = pl.ds(step * LANES, LANES)
                row_hot = row_hots[block, :, spot]
                columns.append(spread([each[step : step + 1] for each in rows], row_hot))
            return total + dot_nt(jnp.concatenate(columns, 1), lane_hots[block])

        total = lax.fori_loop(0, 8, body, jnp.zeros((6 * ROWS, LANES), F32))
        return joined(total)

    def release(totals):
        held = picked(halves(totals), node_lanes[...], node_rows[...], 3, ROWS)
        held = [jnp.concatenate([each, each], 1) for each in held]
        columns = []
        for step in range(8):
            spot = pl.ds(step * LANES, LANES)
            columns.append(spread(held, master_rows[:, spot]))
        added = joined(dot_nt(jnp.concatenate(columns, 1), master_lanes[...]))
        return kept(totals) + added

    def product(left_high, left_low, values, form):
        high = values.astype(BF16)
        low = (values - high.astype(F32)).astype(BF16)
        return form(left_high, high) + form(left_high, low) + form(left_low, high)

    for copy in pending:
        copy.wait()
    import_into(table, recv_first, 0)
    import_into(primal_table, recv_first, 3)

    for sweep in range(SWEEPS):
        if sweep:
            export(owned_of(table), send_ghost.at[2 * sweep - 1], 3)
            for copy in exchange(
                send_ghost.at[2 * sweep - 1], recv_ghost.at[2 * sweep - 1], 2 * sweep, 1
            ):
                copy.wait()
            import_into(table, recv_ghost.at[2 * sweep - 1], 0)
        gather_cells(constrain(table[...]), cells)
        image[...] = modulus * product(stiff_high, stiff_low, cells[...], dot_tn)
        totals = release(scatter_cells(image))
        send, recv = send_ghost.at[2 * sweep], recv_ghost.at[2 * sweep]
        for slot in range(SLOTS):
            for part in range(3):
                spot = part * ROWS + GHOST_ROW + slot
                send[slot, 2 * part : 2 * part + 1, :] = totals[spot : spot + 1, :128]
                send[slot, 2 * part + 1 : 2 * part + 2, :] = totals[spot : spot + 1, 128:]
        pending = exchange(send, recv, 2 * sweep + 1, -1)
        if sweep == 0:
            gather_cells(constrain(primal_table[...]), primal_cells)
            primal_cells[...] = modulus * product(
                stiff_high, stiff_low, primal_cells[...], dot
            )
        for copy in pending:
            copy.wait()
        columns = []
        for slot in range(SLOTS):
            block = arrived(slot, -1, recv[slot])
            rows = [
                jnp.concatenate([block[2 * part : 2 * part + 1], block[2 * part + 1 : 2 * part + 2]], 1)
                for part in range(3)
            ]
            columns.append(spread(rows, list_rows[:, pl.ds(slot * LANES, LANES)]))
        returned = joined(dot_nt(jnp.concatenate(columns, 1), list_lanes[...]))
        for part in range(3):
            owned = pl.ds(part * ROWS, GHOST_ROW)
            span = pl.ds(part * GHOST_ROW, GHOST_ROW)
            applied = (
                totals[part * ROWS : part * ROWS + GHOST_ROW]
                + returned[part * GHOST_ROW : (part + 1) * GHOST_ROW]
            )
            table[owned, :] = table[owned, :] + RELAXATION * inverse[span, :] * (
                source[span, :] - applied
            )

    last = 2 * SWEEPS - 1
    export(owned_of(table), send_ghost.at[last], 3)
    pending = exchange(send_ghost.at[last], recv_ghost.at[last], 2 * SWEEPS, 1)
    for part in range(3):
        for row in range(OWNED):
            adjoint_ref[part, pl.ds(row * LANES, LANES)] = table[part * ROWS + row, :]
    for copy in pending:
        copy.wait()
    import_into(table, recv_ghost.at[last], 0)
    gather_cells(constrain(table[...]), cells)

    applied = primal_cells[...]
    adjoint_cells = cells[...]
    cell_term = jnp.sum(adjoint_cells * (load_ref[...] - applied), axis=0, keepdims=True)
    work = applied * adjoint_cells
    face = lax.broadcasted_iota(jnp.int32, (16, 192), 0)
    node_id = lax.broadcasted_iota(jnp.int32, (16, 192), 1) & 63
    first, second, third = node_id >> 4, (node_id >> 2) & 3, node_id & 3
    axis_index = jnp.where(face < 2, first, jnp.where(face < 4, second, third))
    on_face = jnp.logical_and(face < 6, axis_index == 3 * (face & 1))
    faces = jnp.where(on_face, 1.0, 0.0).astype(BF16)
    work_high = work.astype(BF16)
    work_low = (work - work_high.astype(F32)).astype(BF16)
    flux = (dot(faces, work_high) + dot(faces, work_low))[:8]
    sent = jnp.sum(joined(dot(halves(flux), sub_lanes[...])) * sub_rows[...], axis=0, keepdims=True)
    for slot in range(SLOTS):
        send_sub[slot] = sent[:, slot * 128 : (slot + 1) * 128]
    for copy in exchange(send_sub, recv_sub, 2 * SWEEPS + 1, 1):
        copy.wait()
    received = jnp.concatenate(
        [arrived(slot, 1, recv_sub[slot]) for slot in range(SLOTS)], 1
    )
    stacked = halves(jnp.broadcast_to(received, (8, SLOTS * 128)))
    face_term = dot_nt(stacked, owner_lanes[...])
    face_term = face_term[0:1] + face_term[8:9]
    indicator_ref[...] = (jnp.abs(cell_term) + jnp.abs(face_term)) * (1.0 / 16.0)


def local(
    adjoint_start,
    adjoint_source,
    inverse_diagonal,
    primal_field,
    cell_load,
    modulus,
    stiffness,
    connectivity,
    hang_node,
    hang_master,
    hang_weight,
    ghost_lists,
    subface_cell,
    subface_face,
    subface_owner,
):
    turns = 2 * SWEEPS + 2
    vmem = pltpu.VMEM
    adjoint, indicator = pl.pallas_call(
        kernel,
        out_shape=(
            jax.ShapeDtypeStruct((3, NODES_DEV), F32),
            jax.ShapeDtypeStruct((1, LANES), F32),
        ),
        in_specs=[pl.BlockSpec(memory_space=pltpu.VMEM)] * 15,
        out_specs=(pl.BlockSpec(memory_space=pltpu.VMEM),) * 2,
        scratch_shapes=[
            vmem((3 * ROWS, LANES), F32),
            vmem((3 * ROWS, LANES), F32),
            vmem((3 * GHOST_ROW, LANES), F32),
            vmem((3 * GHOST_ROW, LANES), F32),
            vmem((8, ROWS, 8 * LANES), F32),
            vmem((8, LANES, 8 * LANES), BF16),
            vmem((GHOST_ROW, SLOTS * LANES), F32),
            vmem((LANES, SLOTS * LANES), BF16),
            vmem((ROWS, 16 * 128), F32),
            vmem((LANES, 16 * 128), BF16),
            vmem((ROWS, 128), F32),
            vmem((LANES, 128), BF16),
            vmem((ROWS, LANES), F32),
            vmem((8, SLOTS * 128), F32),
            vmem((LANES, SLOTS * 128), BF16),
            vmem((LANES, SLOTS * 128), BF16),
            vmem((192, LANES), F32),
            vmem((192, LANES), F32),
            vmem((192, LANES), F32),
            vmem((SLOTS, 12, 128), F32),
            vmem((SLOTS, 12, 128), F32),
            vmem((2 * SWEEPS, SLOTS, 6, 128), F32),
            vmem((2 * SWEEPS, SLOTS, 6, 128), F32),
            vmem((SLOTS, 1, 128), F32),
            vmem((SLOTS, 1, 128), F32),
            pltpu.SemaphoreType.DMA((turns, SLOTS)),
            pltpu.SemaphoreType.DMA((turns, SLOTS)),
        ],
        compiler_params=pltpu.CompilerParams(
            collective_id=0, has_side_effects=True, vmem_limit_bytes=56 * 1024 * 1024
        ),
    )(
        adjoint_start,
        adjoint_source,
        inverse_diagonal,
        primal_field,
        cell_load,
        modulus.reshape(1, LANES),
        stiffness,
        connectivity,
        hang_node.reshape(1, 128),
        hang_master,
        hang_weight,
        ghost_lists,
        subface_cell,
        subface_face,
        subface_owner,
    )
    return adjoint, indicator.reshape(LANES)


def solution(mesh):
    wide, flat = P(None, "dom"), P("dom")
    placed = (wide,) * 5 + (flat, P(), wide, flat) + (wide,) * 6
    return jax.shard_map(
        local, mesh=mesh, in_specs=placed, out_specs=(wide, flat), check_vma=False
    )
```

time: 848 us -> 73.8 us (0.09)
  the two profiles are of different devices: /device:TPU:6 before, /device:TPU:1 now
where the time goes in v1:
time: 73.8 us; the launch traced here: 73.6 us
  Pallas kernels  70.8 us (96%)
  local copies, waits for them, and re-layouts  2.13 us (3%)
    pallas_call x1, Pallas kernels, local(): pl.pallas_call(kernel, out_shape=(jax.ShapeDtypeStruct((3, NODES_DEV), F3...  70.8 us
    unnamed x4, local copies, waits for them, and re-layouts  2.13 us

profile of v1, /device:TPU:1, one launch (start us, length us, event | category | flops | bytes accessed | tf_op | source)
XLA Modules:
  0.0 73.6 jit_solution(14859595333882237099)
XLA Ops:
  0.6 70.8 %shard_map.158 = (f32[3,6912]{1,0:T(4,128)}, f32[1,256]{1,0:T(1,128)}) custom-call(f32[3,6912]{1,0:T(4,128)} %start_ref.1, f32[3,6912]{1,0:T(4,128)} %source_ref.1, f32[3,6912]{1,0:T(4,128)} %inverse_ref.1, f32[3,6912]{1,0:T(4,128)} %primal_ref.1, f32[192,256]{1,0:T(8,128)} %load_ref.1, f32[1,256]{1,0:T(1,128)} %bitcast.4, f32[192,192]{1,0:T(8,128)} %stiff_ref.1, ...), custom_call_target="tpu_custom_call" | custom-call | tf_op jit(solution)/shard_map/pallas_call | solution.py:417
  71.5 0.0 copy-start
  71.5 1.6 %copy.19 = f32[3,6912]{1,0:T(4,128)} copy(f32[3,6912]{1,0:T(4,128)} %get-tuple-element.8) | data formatting | bytes 165888
  73.0 0.0 copy-done
  73.0 0.6 copy.20
Async XLA Ops:
  71.5 1.6 %copy-start = (f32[1,256]{1,0:T(1,128)S(1)}, f32[1,256]{1,0:T(1,128)}, u32[]{:S(2)}) copy-start(f32[1,256]{1,0:T(1,128)} %get-tuple-element.5) | copy-start | bytes 3076

commit v2 on v1

v2 whole, which is shorter than its diff:
```python
import jax
import jax.numpy as jnp
from jax import lax
from jax.experimental import pallas as pl
from jax.experimental.pallas import tpu as pltpu
from jax.sharding import PartitionSpec as P

MESH = pl.DeviceIdType.MESH
F32 = jnp.float32
BF16 = jnp.bfloat16

REACH = 4
SLOTS = 2 * REACH
SWEEPS = 2
NODES_DEV = 6912
EXT = 8960
PAD_CODE = 16368
RELAXATION = 0.7
BUILD_FIRST = 4
PRIMAL_FIRST = 4

LANES = 256
OWNED = 27
HANG_ROW = 27
GHOST_ROW = 32
ROWS = 40
OFFSETS = [step + 1 for step in range(REACH)] + [-(step + 1) for step in range(REACH)]


def modulo(values, divisor):
    quotient = ((values.astype(F32) + 0.5) * (1.0 / divisor)).astype(jnp.int32)
    return values - quotient * divisor


def place(slots):
    row = slots >> 8
    return row + jnp.where(row >= OWNED, GHOST_ROW - OWNED, 0), slots & 255


def one_hot(row, count, dtype):
    spots = lax.broadcasted_iota(jnp.int32, (count, row.shape[1]), 0)
    return jnp.where(spots == row, 1.0, 0.0).astype(dtype)


def halves(values):
    high = values.astype(BF16).astype(F32)
    return jnp.concatenate([high, values - high], 0).astype(BF16)


def dot(a, b):
    return jnp.dot(a, b, preferred_element_type=F32)


def dot_nt(a, b):
    return lax.dot_general(a, b, (((1,), (1,)), ((), ())), preferred_element_type=F32)


def dot_tn(a, b):
    return lax.dot_general(a, b, (((0,), (0,)), ((), ())), preferred_element_type=F32)


def joined(values):
    half = values.shape[0] // 2
    return values[:half] + values[half:]


def picked(table, lane_hot, row_hot, parts, rows):
    found = joined(dot(table, lane_hot))
    return [
        jnp.sum(found[part * rows : (part + 1) * rows] * row_hot, axis=0, keepdims=True)
        for part in range(parts)
    ]


def spread(values, row_hot):
    return halves(jnp.concatenate([row_hot * value for value in values], 0))


def kernel(*refs):
    operands, outputs, refs = refs[:15], refs[15:17], refs[17:]
    staged, refs = refs[:15], refs[15:]
    (
        start_ref,
        source_ref,
        inverse_ref,
        primal_ref,
        load_ref,
        modulus_ref,
        stiff_ref,
        connect_ref,
        node_ref,
        master_ref,
        weight_ref,
        lists_ref,
        sub_cell_ref,
        sub_face_ref,
        sub_owner_ref,
    ) = staged
    adjoint_ref, indicator_ref = outputs
    (
        table,
        primal_table,
        source,
        inverse,
        ghosts,
        row_hots,
        lane_hots,
        list_rows,
        list_lanes,
        master_rows,
        master_lanes,
        sub_rows,
        sub_lanes,
        owner_lanes,
        owned_cells,
        cells,
        image,
        primal_cells,
        primal_stack,
        send_first,
        recv_first,
        send_ghost,
        recv_ghost,
        send_sub,
        recv_sub,
        send_sem,
        recv_sem,
        load_sem,
    ) = refs
    me = lax.axis_index("dom")
    count = lax.axis_size("dom")

    def exists(offset):
        other = me + offset
        return jnp.logical_and(other >= 0, other < count)

    barrier = pltpu.get_barrier_semaphore()
    for offset in OFFSETS:

        @pl.when(exists(offset))
        def _(offset=offset):
            pl.semaphore_signal(
                barrier, inc=1, device_id=(me + offset,), device_id_type=MESH
            )

    loads = [
        pltpu.make_async_copy(operands[k], staged[k], load_sem.at[k]) for k in range(15)
    ]
    for k in (11, 0, 3, 7, 8, 9, 10, 1, 2, 6, 5, 12, 13, 14, 4):
        loads[k].start()

    sent = []

    def exchange(send, recv, turn, direction):
        copies = []
        for slot, offset in enumerate(OFFSETS):
            away = direction * offset
            copy = pltpu.make_async_remote_copy(
                src_ref=send.at[slot],
                dst_ref=recv.at[slot],
                send_sem=send_sem.at[turn, slot],
                recv_sem=recv_sem.at[turn, slot],
                device_id=(me + away,),
                device_id_type=MESH,
            )
            pl.when(exists(away))(copy.start)
            copies.append((-away, copy))
            sent.append((away, copy))
        return copies

    def finish(copies):
        for away, copy in copies:
            pl.when(exists(away))(copy.wait_recv)

    def arrived(slot, direction, values):
        return jnp.where(exists(-direction * OFFSETS[slot]), values, 0.0)

    def owned_of(ref):
        return jnp.concatenate(
            [ref[part * ROWS : part * ROWS + GHOST_ROW, :] for part in range(3)], 0
        )

    def fill(ref, rows, values):
        for part in range(3):
            ref[part * rows + OWNED : part * rows + GHOST_ROW, :] = jnp.zeros(
                (GHOST_ROW - OWNED, LANES), F32
            )
            for row in range(OWNED):
                ref[part * rows + row : part * rows + row + 1, :] = values[
                    part : part + 1, row * LANES : (row + 1) * LANES
                ]

    lane_ids = lax.broadcasted_iota(jnp.int32, (SLOTS, LANES), 1)
    loads[11].wait()
    lists = modulo(17 * lists_ref[...] + lane_ids, NODES_DEV)
    for slot in range(SLOTS):
        row = lists[slot : slot + 1]
        spot = pl.ds(slot * LANES, LANES)
        list_lanes[:, spot] = one_hot(row & 255, LANES, BF16)
        list_rows[:, spot] = one_hot(row >> 8, GHOST_ROW, F32)
    loads[0].wait()
    fill(table, GHOST_ROW, start_ref)
    loads[3].wait()
    fill(primal_table, ROWS, primal_ref)

    def export(values, send, parts):
        stacked = halves(values)
        for slot in range(SLOTS):
            spot = pl.ds(slot * LANES, LANES)
            rows = picked(stacked, list_lanes[:, spot], list_rows[:, spot], parts, GHOST_ROW)
            for part in range(parts):
                send[slot, 2 * part : 2 * part + 1, :] = rows[part][:, :128]
                send[slot, 2 * part + 1 : 2 * part + 2, :] = rows[part][:, 128:]

    def imported(recv, first):
        for slot in range(SLOTS):
            block = arrived(slot, 1, recv[slot])
            for part in range(3):
                spot = 2 * (first + part)
                row = pl.ds(part * SLOTS + slot, 1)
                ghosts[row, pl.ds(0, 128)] = block[spot : spot + 1]
                ghosts[row, pl.ds(128, 128)] = block[spot + 1 : spot + 2]
        return ghosts[...]

    export(jnp.concatenate([table[...], owned_of(primal_table)], 0), send_first, 6)

    for k in (7, 8, 9, 10):
        loads[k].wait()
    node = node_ref[...]
    spots = modulo(13 * node, NODES_DEV)
    hang_row = jnp.where(node == PAD_CODE, -1, spots >> 8)
    numbers = (lax.broadcasted_iota(jnp.int32, (1, 128), 1) + 1).astype(F32)
    marks = dot_nt(
        (one_hot(hang_row, GHOST_ROW, F32) * numbers).astype(BF16),
        one_hot(spots & 255, LANES, BF16),
    ).astype(BF16)

    def build(block, carry):
        codes = connect_ref[pl.ds(pl.multiple_of(block * 8, 8), 8), :]
        rows, lanes = place(modulo(17 * codes + 27 * lane_ids, EXT))
        numbers = []
        for step in range(8):
            found = dot(marks, one_hot(lanes[step : step + 1], LANES, BF16))
            found = found * one_hot(rows[step : step + 1], GHOST_ROW, F32)
            numbers.append(jnp.sum(found, axis=0, keepdims=True))
        number = jnp.concatenate(numbers, 0).astype(jnp.int32)
        rows = jnp.where(number > 0, HANG_ROW, rows)
        lanes = jnp.where(number > 0, number - 1, lanes)
        for step in range(8):
            spot = pl.ds(step * LANES, LANES)
            lane_hots[block, :, spot] = one_hot(lanes[step : step + 1], LANES, BF16)
            row_hots[block, :, spot] = one_hot(rows[step : step + 1], ROWS, F32)
        return carry

    lax.fori_loop(0, BUILD_FIRST, build, 0)
    peers = jnp.minimum(me, REACH) + jnp.minimum(count - 1 - me, REACH)
    pl.semaphore_wait(barrier, peers)

    pending = exchange(send_first, recv_first, 0, 1)
    lax.fori_loop(BUILD_FIRST, 8, build, 0)

    hang_ids = lax.broadcasted_iota(jnp.int32, (16, 128), 1)
    row_ids, lanes = place(modulo(17 * master_ref[...] + 8 * hang_ids, EXT))
    weight = weight_ref[...]
    for step in range(16):
        spot = pl.ds(step * 128, 128)
        master_lanes[:, spot] = one_hot(lanes[step : step + 1], LANES, BF16)
        master_rows[:, spot] = (
            one_hot(row_ids[step : step + 1], ROWS, F32) * weight[step : step + 1]
        )

    def masters(values, low, rows):
        stacked = halves(values)
        totals = [jnp.zeros((8, LANES), F32)] * 3
        for step in range(8):
            spot = pl.ds(step * LANES, LANES)
            found = joined(dot(stacked, master_lanes[:, spot]))
            for part in range(3):
                term = found[part * rows : (part + 1) * rows] * master_rows[low : low + rows, spot]
                for group in range(rows // 8):
                    totals[part] = totals[part] + term[group * 8 : group * 8 + 8]
        sums = [jnp.sum(total, axis=0, keepdims=True) for total in totals]
        return [each[:, :128] + each[:, 128:] for each in sums]

    def hanging(first, second):
        rows = [a + b for a, b in zip(first, second)]
        rows = jnp.concatenate(rows + [jnp.zeros((5, 128), F32)], 0)
        return jnp.concatenate([rows, jnp.zeros((8, 128), F32)], 1)

    def gather_rows(stacked, rows, out, first, end):
        def body(block, carry):
            found = [[], [], []]
            for step in range(8):
                spot = pl.ds(step * LANES, LANES)
                values = picked(
                    stacked, lane_hots[block, :, spot], row_hots[block, :rows, spot], 3, rows
                )
                for part in range(3):
                    found[part].append(values[part])
            for part in range(3):
                spot = pl.ds(pl.multiple_of(part * 64 + block * 8, 8), 8)
                out[spot, :] = jnp.concatenate(found[part], 0)
            return carry

        lax.fori_loop(first, end, body, 0)

    def gather_ghosts(values):
        stacked = halves(values)

        def body(block, carry):
            found = [[], [], []]
            for step in range(8):
                spot = pl.ds(step * LANES, LANES)
                rows = joined(dot(stacked, lane_hots[block, :, spot]))
                ghost_hot = row_hots[block, GHOST_ROW:ROWS, spot]
                hang_hot = row_hots[block, HANG_ROW : HANG_ROW + 1, spot]
                hung = rows[24:32] * hang_hot
                for part in range(3):
                    total = jnp.sum(
                        rows[part * 8 : part * 8 + 8] * ghost_hot, axis=0, keepdims=True
                    )
                    found[part].append(total + hung[part : part + 1])
            for part in range(3):
                spot = pl.ds(pl.multiple_of(part * 64 + block * 8, 8), 8)
                cells[spot, :] = owned_cells[spot, :] + jnp.concatenate(found[part], 0)
            return carry

        lax.fori_loop(0, 8, body, 0)

    def image_rows(block):
        return [
            image[pl.ds(pl.multiple_of(part * 64 + block * 8, 8), 8), :] for part in range(3)
        ]

    def scatter_ghosts():
        def body(block, total):
            columns = []
            rows = image_rows(block)
            for step in range(8):
                spot = pl.ds(step * LANES, LANES)
                ghost_hot = row_hots[block, GHOST_ROW:ROWS, spot]
                hang_hot = row_hots[block, HANG_ROW : HANG_ROW + 1, spot]
                values = [each[step : step + 1] for each in rows]
                hung = jnp.concatenate(
                    [value * hang_hot for value in values] + [jnp.zeros((5, LANES), F32)], 0
                )
                columns.append(
                    halves(jnp.concatenate([value * ghost_hot for value in values] + [hung], 0))
                )
            return total + dot_nt(jnp.concatenate(columns, 1), lane_hots[block])

        return joined(lax.fori_loop(0, 8, body, jnp.zeros((64, LANES), F32)))

    def scatter_owned():
        def body(block, total):
            columns = []
            rows = image_rows(block)
            for step in range(8):
                spot = pl.ds(step * LANES, LANES)
                row_hot = row_hots[block, :GHOST_ROW, spot]
                columns.append(spread([each[step : step + 1] for each in rows], row_hot))
            return total + dot_nt(jnp.concatenate(columns, 1), lane_hots[block])

        return joined(lax.fori_loop(0, 8, body, jnp.zeros((6 * GHOST_ROW, LANES), F32)))

    def released(held, low, rows):
        columns = []
        for step in range(8):
            spot = pl.ds(step * LANES, LANES)
            columns.append(spread(held, master_rows[low : low + rows, spot]))
        return joined(dot_nt(jnp.concatenate(columns, 1), master_lanes[...]))

    def product(values, form):
        high = values.astype(BF16)
        low = (values - high.astype(F32)).astype(BF16)
        return form(stiff_high, high) + form(stiff_high, low) + form(stiff_low, high)

    owned_masters = masters(table[...], 0, GHOST_ROW)
    gather_rows(halves(table[...]), GHOST_ROW, owned_cells, 0, 8)
    for k in (1, 2, 6, 5):
        loads[k].wait()
    stiff = stiff_ref[...]
    stiff_high = stiff.astype(BF16)
    stiff_low = (stiff - stiff_high.astype(F32)).astype(BF16)
    modulus = modulus_ref[...]
    fill(source, GHOST_ROW, source_ref)
    fill(inverse, GHOST_ROW, inverse_ref)

    recv = recv_first
    for sweep in range(SWEEPS):
        finish(pending)
        values = imported(recv, 0)
        hung = hanging(owned_masters, masters(values, GHOST_ROW, 8))
        gather_ghosts(jnp.concatenate([values, hung], 0))
        image[...] = modulus * product(cells[...], dot_tn)
        totals = scatter_ghosts()
        held = [
            jnp.concatenate([totals[24 + part : 25 + part, :128]] * 2, 1) for part in range(3)
        ]
        totals = totals[:24] + released(held, GHOST_ROW, 8)
        send, recv = send_ghost.at[2 * sweep], recv_ghost.at[2 * sweep]
        for slot in range(SLOTS):
            for part in range(3):
                spot = part * SLOTS + slot
                send[slot, 2 * part : 2 * part + 1, :] = totals[spot : spot + 1, :128]
                send[slot, 2 * part + 1 : 2 * part + 2, :] = totals[spot : spot + 1, 128:]
        pending = exchange(send, recv, 2 * sweep + 1, -1)

        totals = scatter_owned() + released(held, 0, GHOST_ROW)
        if sweep == 0:
            values = imported(recv_first, 3)
            hung = hanging(
                masters(owned_of(primal_table), 0, GHOST_ROW), masters(values, GHOST_ROW, 8)
            )
            for part in range(3):
                row = part * ROWS
                primal_table[row + HANG_ROW : row + HANG_ROW + 1, :] = hung[part : part + 1]
                primal_table[row + GHOST_ROW : row + ROWS, :] = values[
                    part * SLOTS : (part + 1) * SLOTS
                ]
            primal_stack[...] = halves(primal_table[...])
            gather_rows(primal_stack[...], ROWS, primal_cells, 0, PRIMAL_FIRST)
        if sweep == SWEEPS - 1:
            primal_cells[...] = modulus * product(primal_cells[...], dot)
            for k in (12, 13, 14):
                loads[k].wait()
            for slot in range(SLOTS):
                spot = pl.ds(slot * 128, 128)
                sub_lanes[:, spot] = one_hot(sub_cell_ref[slot : slot + 1, :], LANES, BF16)
                sub_rows[:, spot] = one_hot(sub_face_ref[slot : slot + 1, :], 8, F32)
                owner_lanes[:, spot] = one_hot(sub_owner_ref[slot : slot + 1, :], LANES, BF16)
        finish(pending)
        columns = []
        for slot in range(SLOTS):
            block = arrived(slot, -1, recv[slot])
            rows = [
                jnp.concatenate(
                    [block[2 * part : 2 * part + 1], block[2 * part + 1 : 2 * part + 2]], 1
                )
                for part in range(3)
            ]
            columns.append(spread(rows, list_rows[:, pl.ds(slot * LANES, LANES)]))
        returned = joined(dot_nt(jnp.concatenate(columns, 1), list_lanes[...]))
        table[...] = table[...] + RELAXATION * inverse[...] * (
            source[...] - (totals + returned)
        )
        send, recv = send_ghost.at[2 * sweep + 1], recv_ghost.at[2 * sweep + 1]
        export(table[...], send, 3)
        pending = exchange(send, recv, 2 * sweep + 2, 1)

        owned_masters = masters(table[...], 0, GHOST_ROW)
        gather_rows(halves(table[...]), GHOST_ROW, owned_cells, 0, 8)
        if sweep == 0:
            gather_rows(primal_stack[...], ROWS, primal_cells, PRIMAL_FIRST, 8)

    for part in range(3):
        for row in range(OWNED):
            spot = part * GHOST_ROW + row
            adjoint_ref[part : part + 1, row * LANES : (row + 1) * LANES] = table[
                spot : spot + 1, :
            ]
    loads[4].wait()
    face = lax.broadcasted_iota(jnp.int32, (16, 192), 0)
    node_id = lax.broadcasted_iota(jnp.int32, (16, 192), 1) & 63
    first, second, third = node_id >> 4, (node_id >> 2) & 3, node_id & 3
    axis_index = jnp.where(face < 2, first, jnp.where(face < 4, second, third))
    on_face = jnp.logical_and(face < 6, axis_index == 3 * (face & 1))
    faces = jnp.where(on_face, 1.0, 0.0).astype(BF16)

    finish(pending)
    values = imported(recv, 0)
    hung = hanging(owned_masters, masters(values, GHOST_ROW, 8))
    gather_ghosts(jnp.concatenate([values, hung], 0))
    applied = primal_cells[...]
    work = applied * cells[...]
    work_high = work.astype(BF16)
    work_low = (work - work_high.astype(F32)).astype(BF16)
    flux = (dot(faces, work_high) + dot(faces, work_low))[:8]
    found = joined(dot(halves(flux), sub_lanes[...])) * sub_rows[...]
    found = jnp.sum(found, axis=0, keepdims=True)
    for slot in range(SLOTS):
        send_sub[slot] = found[:, slot * 128 : (slot + 1) * 128]
    pending = exchange(send_sub, recv_sub, 2 * SWEEPS + 1, 1)
    cell_term = jnp.sum(cells[...] * (load_ref[...] - applied), axis=0, keepdims=True)
    finish(pending)
    received = jnp.concatenate(
        [arrived(slot, 1, recv_sub[slot]) for slot in range(SLOTS)], 1
    )
    stacked = halves(jnp.broadcast_to(received, (8, SLOTS * 128)))
    face_term = dot_nt(stacked, owner_lanes[...])
    face_term = face_term[0:1] + face_term[8:9]
    indicator_ref[...] = (jnp.abs(cell_term) + jnp.abs(face_term)) * (1.0 / 16.0)
    for away, copy in sent:
        pl.when(exists(away))(copy.wait_send)


def local(
    adjoint_start,
    adjoint_source,
    inverse_diagonal,
    primal_field,
    cell_load,
    modulus,
    stiffness,
    connectivity,
    hang_node,
    hang_master,
    hang_weight,
    ghost_lists,
    subface_cell,
    subface_face,
    subface_owner,
):
    turns = 2 * SWEEPS + 2
    operands = (
        adjoint_start,
        adjoint_source,
        inverse_diagonal,
        primal_field,
        cell_load,
        modulus.reshape(1, LANES),
        stiffness,
        connectivity,
        hang_node.reshape(1, 128),
        hang_master,
        hang_weight,
        ghost_lists,
        subface_cell,
        subface_face,
        subface_owner,
    )
    vmem = pltpu.VMEM
    adjoint, indicator = pl.pallas_call(
        kernel,
        out_shape=(
            jax.ShapeDtypeStruct((3, NODES_DEV), F32),
            jax.ShapeDtypeStruct((1, LANES), F32),
        ),
        in_specs=[pl.BlockSpec(memory_space=pl.ANY)] * 15,
        out_specs=(pl.BlockSpec(memory_space=pltpu.VMEM),) * 2,
        scratch_shapes=[vmem(each.shape, each.dtype) for each in operands]
        + [
            vmem((3 * GHOST_ROW, LANES), F32),
            vmem((3 * ROWS, LANES), F32),
            vmem((3 * GHOST_ROW, LANES), F32),
            vmem((3 * GHOST_ROW, LANES), F32),
            vmem((3 * SLOTS, LANES), F32),
            vmem((8, ROWS, 8 * LANES), F32),
            vmem((8, LANES, 8 * LANES), BF16),
            vmem((GHOST_ROW, SLOTS * LANES), F32),
            vmem((LANES, SLOTS * LANES), BF16),
            vmem((ROWS, 16 * 128), F32),
            vmem((LANES, 16 * 128), BF16),
            vmem((8, SLOTS * 128), F32),
            vmem((LANES, SLOTS * 128), BF16),
            vmem((LANES, SLOTS * 128), BF16),
            vmem((192, LANES), F32),
            vmem((192, LANES), F32),
            vmem((192, LANES), F32),
            vmem((192, LANES), F32),
            vmem((6 * ROWS, LANES), BF16),
            vmem((SLOTS, 12, 128), F32),
            vmem((SLOTS, 12, 128), F32),
            vmem((2 * SWEEPS, SLOTS, 6, 128), F32),
            vmem((2 * SWEEPS, SLOTS, 6, 128), F32),
            vmem((SLOTS, 1, 128), F32),
            vmem((SLOTS, 1, 128), F32),
            pltpu.SemaphoreType.DMA((turns, SLOTS)),
            pltpu.SemaphoreType.DMA((turns, SLOTS)),
            pltpu.SemaphoreType.DMA((15,)),
        ],
        compiler_params=pltpu.CompilerParams(
            collective_id=0, has_side_effects=True, vmem_limit_bytes=56 * 1024 * 1024
        ),
    )(*operands)
    return adjoint, indicator.reshape(LANES)


def solution(mesh):
    wide, flat = P(None, "dom"), P("dom")
    placed = (wide,) * 5 + (flat, P(), wide, flat) + (wide,) * 6
    return jax.shard_map(
        local, mesh=mesh, in_specs=placed, out_specs=(wide, flat), check_vma=False
    )
```

time: 73.8 us -> 67.2 us (0.911)
  the two profiles are of different devices: /device:TPU:1 before, /device:TPU:6 now
where the time goes in v2:
time: 67.2 us; the launch traced here: 67.1 us
  Pallas kernels  64.3 us (96%)
  local copies, waits for them, and re-layouts  2.13 us (3%)
    pallas_call x1, Pallas kernels, local(): pl.pallas_call(kernel, out_shape=(jax.ShapeDtypeStruct((3, NODES_DEV), F3...  64.3 us
    unnamed x4, local copies, waits for them, and re-layouts  2.13 us

profile of v2, /device:TPU:6, one launch (start us, length us, event | category | flops | bytes accessed | tf_op | source)
XLA Modules:
  0.0 67.1 jit_solution(17373528735008708724)
XLA Ops:
  0.6 64.3 %shard_map.158 = (f32[3,6912]{1,0:T(4,128)}, f32[1,256]{1,0:T(1,128)}) custom-call(f32[3,6912]{1,0:T(4,128)} %refs_0_.1, f32[3,6912]{1,0:T(4,128)} %refs_1_.1, f32[3,6912]{1,0:T(4,128)} %refs_2_.1, f32[3,6912]{1,0:T(4,128)} %refs_3_.1, f32[192,256]{1,0:T(8,128)} %refs_4_.1, f32[1,256]{1,0:T(1,128)} %bitcast.4, f32[192,192]{1,0:T(8,128)} %refs_6_.1, ...), custom_call_target="tpu_custom_call" | custom-call | tf_op jit(solution)/shard_map/pallas_call | solution.py:533
  65.0 0.0 copy-start
  65.0 1.6 %copy.19 = f32[3,6912]{1,0:T(4,128)} copy(f32[3,6912]{1,0:T(4,128)} %get-tuple-element.8) | data formatting | bytes 165888
  66.5 0.0 copy-done
  66.5 0.6 copy.20
Async XLA Ops:
  65.0 1.6 %copy-start = (f32[1,256]{1,0:T(1,128)S(1)}, f32[1,256]{1,0:T(1,128)}, u32[]{:S(2)}) copy-start(f32[1,256]{1,0:T(1,128)} %get-tuple-element.5) | copy-start | bytes 3076

commit v3 on v2

v3 whole, which is shorter than its diff:
```python
import jax
import jax.numpy as jnp
from jax import lax
from jax.experimental import pallas as pl
from jax.experimental.pallas import tpu as pltpu
from jax.sharding import PartitionSpec as P

MESH = pl.DeviceIdType.MESH
F32 = jnp.float32
BF16 = jnp.bfloat16

REACH = 4
SLOTS = 2 * REACH
SWEEPS = 2
NODES_DEV = 6912
EXT = 8960
PAD_CODE = 16368
RELAXATION = 0.7
BUILD_FIRST = 4
PRIMAL_CUTS = (0, 1, 3, 4)

LANES = 128
OWNED = NODES_DEV // LANES
HANG_ROW = OWNED
STRIDE = 64
GHOSTS = 2 * SLOTS
OFFSETS = [step + 1 for step in range(REACH)] + [-(step + 1) for step in range(REACH)]


def modulo(values, divisor):
    quotient = ((values.astype(F32) + 0.5) * (1.0 / divisor)).astype(jnp.int32)
    return values - quotient * divisor


def place(slots):
    row = slots >> 7
    return row + jnp.where(row >= OWNED, STRIDE - OWNED, 0), slots & 127


def one_hot(row, count, dtype, low=0):
    spots = lax.broadcasted_iota(jnp.int32, (count, row.shape[1]), 0) + low
    return jnp.where(spots == row, 1.0, 0.0).astype(dtype)


def halves(values):
    high = values.astype(BF16).astype(F32)
    return jnp.concatenate([high, values - high], 0).astype(BF16)


def dot(a, b):
    return jnp.dot(a, b, preferred_element_type=F32)


def dot_nt(a, b):
    return lax.dot_general(a, b, (((1,), (1,)), ((), ())), preferred_element_type=F32)


def dot_tn(a, b):
    return lax.dot_general(a, b, (((0,), (0,)), ((), ())), preferred_element_type=F32)


def joined(values):
    half = values.shape[0] // 2
    return values[:half] + values[half:]


def looked_up(rows_of, spots, parts, start=None):
    found = start or [[jnp.zeros((8, LANES), F32)] * parts for _ in spots]
    found = [list(each) for each in found]
    for each, (rows, lanes) in zip(found, spots):
        for number, row_of in rows_of:
            hit = rows == number
            for part in range(parts):
                table = jnp.broadcast_to(row_of(part), (8, LANES))
                value = jnp.take_along_axis(table, lanes, axis=1, mode="promise_in_bounds")
                each[part] = jnp.where(hit, value, each[part])
    return found


def spread(values, row_hot):
    return halves(jnp.concatenate([row_hot * value for value in values], 0))


def kernel(*refs):
    operands, outputs, refs = refs[:15], refs[15:17], refs[17:]
    staged, refs = refs[:15], refs[15:]
    (
        start_ref,
        source_ref,
        inverse_ref,
        primal_ref,
        load_ref,
        modulus_ref,
        stiff_ref,
        connect_ref,
        node_ref,
        master_ref,
        weight_ref,
        lists_ref,
        sub_cell_ref,
        sub_face_ref,
        sub_owner_ref,
    ) = staged
    adjoint_ref, indicator_ref = outputs
    (
        table,
        primal_table,
        source,
        inverse,
        row_hots,
        ghost_hots,
        hang_hots,
        lane_hots,
        cell_rows,
        cell_lanes,
        list_hots,
        list_lanes,
        master_hots,
        master_lanes,
        owner_lanes,
        owned_cells,
        cells,
        image,
        primal_cells,
        send_first,
        recv_first,
        send_ghost,
        recv_ghost,
        send_sub,
        recv_sub,
        send_sem,
        recv_sem,
        load_sem,
    ) = refs
    me = lax.axis_index("dom")
    count = lax.axis_size("dom")

    def exists(offset):
        other = me + offset
        return jnp.logical_and(other >= 0, other < count)

    barrier = pltpu.get_barrier_semaphore()
    for offset in OFFSETS:

        @pl.when(exists(offset))
        def _(offset=offset):
            pl.semaphore_signal(
                barrier, inc=1, device_id=(me + offset,), device_id_type=MESH
            )

    loads = [
        pltpu.make_async_copy(operands[k], staged[k], load_sem.at[k]) for k in range(15)
    ]
    for k in (11, 0, 3, 7, 8, 9, 10, 1, 2, 6, 5, 12, 13, 14, 4):
        loads[k].start()

    sent = []

    def exchange(send, recv, turn, direction):
        copies = []
        for slot, offset in enumerate(OFFSETS):
            away = direction * offset
            copy = pltpu.make_async_remote_copy(
                src_ref=send.at[slot],
                dst_ref=recv.at[slot],
                send_sem=send_sem.at[turn, slot],
                recv_sem=recv_sem.at[turn, slot],
                device_id=(me + away,),
                device_id_type=MESH,
            )
            pl.when(exists(away))(copy.start)
            copies.append((-away, copy))
            sent.append((away, copy))
        return copies

    def finish(copies):
        for away, copy in copies:
            pl.when(exists(away))(copy.wait_recv)

    for slot, offset in enumerate(OFFSETS):

        @pl.when(jnp.logical_not(exists(-offset)))
        def _(slot=slot):
            recv_first[slot] = jnp.zeros((12, LANES), F32)
            recv_sub[slot] = jnp.zeros((1, LANES), F32)
            for turn in range(SWEEPS):
                recv_ghost[2 * turn + 1, slot] = jnp.zeros((6, LANES), F32)

        @pl.when(jnp.logical_not(exists(offset)))
        def _(slot=slot):
            for turn in range(SWEEPS):
                recv_ghost[2 * turn, slot] = jnp.zeros((6, LANES), F32)

    def fill(ref, values):
        for part in range(3):
            low = part * STRIDE
            ref[low + OWNED - 6 : low + STRIDE, :] = jnp.zeros((STRIDE - OWNED + 6, LANES), F32)
            for row in range(OWNED):
                ref[low + row : low + row + 1, :] = values[
                    part : part + 1, row * LANES : (row + 1) * LANES
                ]

    def owned_rows(ref):
        def row_of(row):
            return lambda part: ref[part * STRIDE + row : part * STRIDE + row + 1, :]

        return [(row, row_of(row)) for row in range(OWNED)]

    def ghost_rows(recv, first=0):
        def row_of(row):
            spot = row % 2
            return lambda part: recv[
                row // 2, 2 * (first + part) + spot : 2 * (first + part) + spot + 1, :
            ]

        return [(STRIDE + row, row_of(row)) for row in range(GHOSTS)]

    lane_ids = lax.broadcasted_iota(jnp.int32, (SLOTS, 256), 1)
    loads[11].wait()
    lists = modulo(17 * lists_ref[...] + lane_ids, NODES_DEV)
    list_spots = [
        (lists[:, LANES * half : LANES * (half + 1)] >> 7, lists[:, LANES * half : LANES * (half + 1)] & 127)
        for half in range(2)
    ]
    loads[0].wait()
    fill(table, start_ref)

    def export(ref, send, first=0):
        found = looked_up(owned_rows(ref), list_spots, 3)
        for part in range(3):
            for half in range(2):
                spot = 2 * (first + part) + half
                for slot in range(SLOTS):
                    send[slot, spot : spot + 1, :] = found[half][part][slot : slot + 1]

    export(table, send_first)
    loads[3].wait()
    fill(primal_table, primal_ref)
    export(primal_table, send_first, 3)

    for k in (7, 8, 9, 10):
        loads[k].wait()
    node = node_ref[...]
    spots = modulo(13 * node, NODES_DEV)
    hang_row = jnp.where(node == PAD_CODE, -1, spots >> 7)
    numbers = (lax.broadcasted_iota(jnp.int32, (1, LANES), 1) + 1).astype(F32)
    source[: STRIDE, :] = dot_nt(
        (one_hot(hang_row, STRIDE, F32) * numbers).astype(BF16),
        one_hot(spots & 127, LANES, BF16),
    )

    def build(block, carry):
        span = pl.ds(pl.multiple_of(block * 8, 8), 8)
        codes = connect_ref[span, :]
        rows, lanes = place(modulo(17 * codes + 27 * lane_ids, EXT))
        pairs = [(rows[:, :LANES], lanes[:, :LANES]), (rows[:, LANES:], lanes[:, LANES:])]
        number = [each[0] for each in looked_up(owned_rows(source), pairs, 1)]
        number = jnp.concatenate(number, 1).astype(jnp.int32)
        rows = jnp.where(number > 0, HANG_ROW, rows)
        lanes = jnp.where(number > 0, number - 1, lanes)
        cell_rows[span, :] = rows
        cell_lanes[span, :] = lanes
        hang_hots[span, :] = jnp.where(rows == HANG_ROW, 1.0, 0.0)
        for step in range(8):
            spot = pl.ds(step * 256, 256)
            lane_hots[block, :, spot] = one_hot(lanes[step : step + 1], LANES, BF16)
            row_hots[block, :, spot] = one_hot(rows[step : step + 1], STRIDE, BF16)
            ghost_hots[block, :, spot] = one_hot(rows[step : step + 1], GHOSTS, F32, STRIDE)
        return carry

    lax.fori_loop(0, BUILD_FIRST, build, 0)
    peers = jnp.minimum(me, REACH) + jnp.minimum(count - 1 - me, REACH)
    pl.semaphore_wait(barrier, peers)
    pending = exchange(send_first, recv_first, 0, 1)
    lax.fori_loop(BUILD_FIRST, 8, build, 0)

    hang_ids = lax.broadcasted_iota(jnp.int32, (16, LANES), 1)
    rows, lanes = place(modulo(17 * master_ref[...] + 8 * hang_ids, EXT))
    weight = weight_ref[...]
    master_spots = [(rows[:8], lanes[:8]), (rows[8:], lanes[8:])]
    for step in range(16):
        spot = pl.ds(step * LANES, LANES)
        master_lanes[:, spot] = one_hot(lanes[step : step + 1], LANES, BF16)
        master_hots[:, spot] = (
            one_hot(rows[step : step + 1], STRIDE + GHOSTS, F32) * weight[step : step + 1]
        )

    def hanging(found):
        rows = []
        for part in range(3):
            total = found[0][part] * weight[:8] + found[1][part] * weight[8:]
            rows.append(jnp.sum(total, axis=0, keepdims=True))
        return rows

    def hang_rows(values):
        return [(HANG_ROW, lambda part: values[part])]

    def gather_cells(rows_of, base, out, first, end):
        def body(group, carry):
            spots, spans = [], []
            for block in range(2):
                for half in range(2):
                    low = pl.multiple_of(group * 16 + block * 8, 8)
                    lane = pl.ds(half * LANES, LANES)
                    spots.append((cell_rows[pl.ds(low, 8), lane], cell_lanes[pl.ds(low, 8), lane]))
                    spans.append((low, lane))

            def span(part, where):
                return pl.ds(pl.multiple_of(part * 64 + where[0], 8), 8), where[1]

            start = None
            if base is not None:
                start = [[base[span(part, where)] for part in range(3)] for where in spans]
            found = looked_up(rows_of, spots, 3, start)
            for values, where in zip(found, spans):
                for part in range(3):
                    out[span(part, where)] = values[part]
            return carry

        lax.fori_loop(first, end, body, 0)

    def image_rows(block):
        return [
            image[pl.ds(pl.multiple_of(part * 64 + block * 8, 8), 8), :] for part in range(3)
        ]

    def scatter_ghosts():
        def body(block, total):
            columns = []
            rows = image_rows(block)
            hang_hot = hang_hots[pl.ds(pl.multiple_of(block * 8, 8), 8), :]
            hung = [each * hang_hot for each in rows]
            for step in range(8):
                spot = pl.ds(step * 256, 256)
                ghost_hot = ghost_hots[block, :, spot]
                columns.append(
                    halves(
                        jnp.concatenate(
                            [each[step : step + 1] * ghost_hot for each in rows]
                            + [each[step : step + 1] for each in hung]
                            + [jnp.zeros((5, 256), F32)],
                            0,
                        )
                    )
                )
            return total + dot_nt(jnp.concatenate(columns, 1), lane_hots[block])

        zero = jnp.zeros((2 * (3 * GHOSTS + 8), LANES), F32)
        return joined(lax.fori_loop(0, 8, body, zero))

    def scatter_owned():
        def body(block, total):
            columns = []
            rows = image_rows(block)
            high = [each.astype(BF16).astype(F32) for each in rows]
            values = high + [a - b for a, b in zip(rows, high)]
            for step in range(8):
                spot = pl.ds(step * 256, 256)
                row_hot = row_hots[block, :, spot]
                column = []
                for each in values:
                    tile = jnp.broadcast_to(each[step : step + 1], (16, 256)).astype(BF16)
                    column.append(row_hot * jnp.concatenate([tile] * (STRIDE // 16), 0))
                columns.append(jnp.concatenate(column, 0))
            return total + dot_nt(jnp.concatenate(columns, 1), lane_hots[block])

        return joined(lax.fori_loop(0, 8, body, jnp.zeros((6 * STRIDE, LANES), F32)))

    def released(held, low, rows):
        columns = []
        for step in range(8):
            spot = pl.ds(step * 256, 256)
            columns.append(spread(held, master_hots[low : low + rows, spot]))
        return joined(dot_nt(jnp.concatenate(columns, 1), master_lanes[...]))

    def product(values, form):
        high = values.astype(BF16)
        low = (values - high.astype(F32)).astype(BF16)
        return form(stiff_high, high) + form(stiff_high, low) + form(stiff_low, high)

    owned_masters = looked_up(owned_rows(table), master_spots, 3)
    gather_cells(owned_rows(table), None, owned_cells, 0, 4)
    for k in (1, 2, 6, 5):
        loads[k].wait()
    stiff = stiff_ref[...]
    stiff_high = stiff.astype(BF16)
    stiff_low = (stiff - stiff_high.astype(F32)).astype(BF16)
    modulus = modulus_ref[...]
    fill(source, source_ref)
    fill(inverse, inverse_ref)
    for slot in range(SLOTS):
        row = lists[slot : slot + 1]
        spot = pl.ds(slot * 256, 256)
        list_lanes[:, spot] = one_hot(row & 127, LANES, BF16)
        list_hots[:, spot] = one_hot(row >> 7, STRIDE, F32)

    recv, first = recv_first, 0
    for sweep in range(SWEEPS):
        finish(pending)
        hung = hanging(looked_up(ghost_rows(recv), master_spots, 3, owned_masters))
        gather_cells(ghost_rows(recv) + hang_rows(hung), owned_cells, cells, 0, 4)
        image[...] = modulus * product(cells[...], dot_tn)
        totals = scatter_ghosts()
        held = [
            jnp.concatenate([totals[3 * GHOSTS + part : 3 * GHOSTS + part + 1]] * 2, 1)
            for part in range(3)
        ]
        totals = totals[: 3 * GHOSTS] + released(held, STRIDE, GHOSTS)
        send, recv = send_ghost.at[2 * sweep], recv_ghost.at[2 * sweep]
        for slot in range(SLOTS):
            for part in range(3):
                spot = part * GHOSTS + 2 * slot
                send[slot, 2 * part : 2 * part + 2, :] = totals[spot : spot + 2]
        pending = exchange(send, recv, 2 * sweep + 1, -1)

        totals = scatter_owned() + released(held, 0, STRIDE)
        if sweep == 0:
            primal_rows = owned_rows(primal_table) + ghost_rows(recv_first, 3)
            primal_rows += hang_rows(hanging(looked_up(primal_rows, master_spots, 3)))
        if sweep == SWEEPS - 1:
            primal_cells[...] = modulus * product(primal_cells[...], dot)
            for k in (12, 13, 14):
                loads[k].wait()
            for slot in range(SLOTS):
                owner_lanes[:, pl.ds(slot * LANES, LANES)] = one_hot(
                    sub_owner_ref[slot : slot + 1, :], 256, BF16
                )
        else:
            gather_cells(
                primal_rows, None, primal_cells, PRIMAL_CUTS[2 * sweep], PRIMAL_CUTS[2 * sweep + 1]
            )
        finish(pending)
        columns = []
        for slot in range(SLOTS):
            rows = [
                jnp.concatenate(
                    [recv[slot, 2 * part : 2 * part + 1, :], recv[slot, 2 * part + 1 : 2 * part + 2, :]],
                    1,
                )
                for part in range(3)
            ]
            columns.append(spread(rows, list_hots[:, pl.ds(slot * 256, 256)]))
        returned = joined(dot_nt(jnp.concatenate(columns, 1), list_lanes[...]))
        table[...] = table[...] + RELAXATION * inverse[...] * (
            source[...] - (totals + returned)
        )
        send, recv = send_ghost.at[2 * sweep + 1], recv_ghost.at[2 * sweep + 1]
        export(table, send)
        pending = exchange(send, recv, 2 * sweep + 2, 1)

        owned_masters = looked_up(owned_rows(table), master_spots, 3)
        gather_cells(owned_rows(table), None, owned_cells, 0, 4)
        if sweep == 0:
            gather_cells(primal_rows, None, primal_cells, PRIMAL_CUTS[1], 4)

    for part in range(3):
        for row in range(OWNED):
            spot = part * STRIDE + row
            adjoint_ref[part : part + 1, row * LANES : (row + 1) * LANES] = table[
                spot : spot + 1, :
            ]
    loads[4].wait()
    face = lax.broadcasted_iota(jnp.int32, (16, 192), 0)
    node_id = lax.broadcasted_iota(jnp.int32, (16, 192), 1) & 63
    first, second, third = node_id >> 4, (node_id >> 2) & 3, node_id & 3
    axis_index = jnp.where(face < 2, first, jnp.where(face < 4, second, third))
    on_face = jnp.logical_and(face < 6, axis_index == 3 * (face & 1))
    faces = jnp.where(on_face, 1.0, 0.0).astype(BF16)
    sub_cell = sub_cell_ref[...]
    sub_spot = (2 * sub_face_ref[...] + (sub_cell >> 7), sub_cell & 127)

    finish(pending)
    hung = hanging(looked_up(ghost_rows(recv), master_spots, 3, owned_masters))
    gather_cells(ghost_rows(recv) + hang_rows(hung), owned_cells, cells, 0, 4)
    applied = primal_cells[...]
    work = applied * cells[...]
    work_high = work.astype(BF16)
    work_low = (work - work_high.astype(F32)).astype(BF16)
    flux = dot(faces, work_high) + dot(faces, work_low)

    def flux_row(face, half):
        return lambda part: flux[face : face + 1, half * LANES : (half + 1) * LANES]

    flux_rows = [(2 * face + half, flux_row(face, half)) for face in range(6) for half in range(2)]
    found = looked_up(flux_rows, [sub_spot], 1)[0][0]
    for slot in range(SLOTS):
        send_sub[slot] = found[slot : slot + 1]
    pending = exchange(send_sub, recv_sub, 2 * SWEEPS + 1, 1)
    cell_term = jnp.sum(cells[...] * (load_ref[...] - applied), axis=0, keepdims=True)
    finish(pending)
    received = jnp.concatenate([recv_sub[slot] for slot in range(SLOTS)], 1)
    stacked = halves(jnp.broadcast_to(received, (8, SLOTS * LANES)))
    face_term = dot_nt(stacked, owner_lanes[...])
    face_term = face_term[0:1] + face_term[8:9]
    indicator_ref[...] = (jnp.abs(cell_term) + jnp.abs(face_term)) * (1.0 / 16.0)
    for away, copy in sent:
        pl.when(exists(away))(copy.wait_send)


def local(
    adjoint_start,
    adjoint_source,
    inverse_diagonal,
    primal_field,
    cell_load,
    modulus,
    stiffness,
    connectivity,
    hang_node,
    hang_master,
    hang_weight,
    ghost_lists,
    subface_cell,
    subface_face,
    subface_owner,
):
    turns = 2 * SWEEPS + 2
    operands = (
        adjoint_start,
        adjoint_source,
        inverse_diagonal,
        primal_field,
        cell_load,
        modulus.reshape(1, 256),
        stiffness,
        connectivity,
        hang_node.reshape(1, 128),
        hang_master,
        hang_weight,
        ghost_lists,
        subface_cell,
        subface_face,
        subface_owner,
    )
    vmem = pltpu.VMEM
    adjoint, indicator = pl.pallas_call(
        kernel,
        out_shape=(
            jax.ShapeDtypeStruct((3, NODES_DEV), F32),
            jax.ShapeDtypeStruct((1, 256), F32),
        ),
        in_specs=[pl.BlockSpec(memory_space=pl.ANY)] * 15,
        out_specs=(pl.BlockSpec(memory_space=pltpu.VMEM),) * 2,
        scratch_shapes=[vmem(each.shape, each.dtype) for each in operands]
        + [
            vmem((3 * STRIDE, LANES), F32),
            vmem((3 * STRIDE, LANES), F32),
            vmem((3 * STRIDE, LANES), F32),
            vmem((3 * STRIDE, LANES), F32),
            vmem((8, STRIDE, 8 * 256), BF16),
            vmem((8, GHOSTS, 8 * 256), F32),
            vmem((64, 256), F32),
            vmem((8, LANES, 8 * 256), BF16),
            vmem((64, 256), jnp.int32),
            vmem((64, 256), jnp.int32),
            vmem((STRIDE, SLOTS * 256), F32),
            vmem((LANES, SLOTS * 256), BF16),
            vmem((STRIDE + GHOSTS, 16 * LANES), F32),
            vmem((LANES, 16 * LANES), BF16),
            vmem((256, SLOTS * LANES), BF16),
            vmem((192, 256), F32),
            vmem((192, 256), F32),
            vmem((192, 256), F32),
            vmem((192, 256), F32),
            vmem((SLOTS, 12, LANES), F32),
            vmem((SLOTS, 12, LANES), F32),
            vmem((2 * SWEEPS, SLOTS, 6, LANES), F32),
            vmem((2 * SWEEPS, SLOTS, 6, LANES), F32),
            vmem((SLOTS, 1, LANES), F32),
            vmem((SLOTS, 1, LANES), F32),
            pltpu.SemaphoreType.DMA((turns, SLOTS)),
            pltpu.SemaphoreType.DMA((turns, SLOTS)),
            pltpu.SemaphoreType.DMA((15,)),
        ],
        compiler_params=pltpu.CompilerParams(
            collective_id=0, has_side_effects=True, vmem_limit_bytes=56 * 1024 * 1024
        ),
    )(*operands)
    return adjoint, indicator.reshape(256)


def solution(mesh):
    wide, flat = P(None, "dom"), P("dom")
    placed = (wide,) * 5 + (flat, P(), wide, flat) + (wide,) * 6
    return jax.shard_map(
        local, mesh=mesh, in_specs=placed, out_specs=(wide, flat), check_vma=False
    )
```

time: 67.2 us -> 59.2 us (0.88)
  Pallas kernels: 64.3 us -> 56.3 us
    pallas_call x1, Pallas kernels: 64.3 us -> 56.3 us  [local(): pl.pallas_call(kernel, out_shape=(jax.ShapeDtypeStruct((3, NODES_DEV), F3...]
where the time goes in v3:
time: 59.2 us; the launch traced here: 59.1 us
  Pallas kernels  56.3 us (95%)
  local copies, waits for them, and re-layouts  2.13 us (4%)
  between operations  0.65 us (1%)
    pallas_call x1, Pallas kernels, local(): pl.pallas_call(kernel, out_shape=(jax.ShapeDtypeStruct((3, NODES_DEV), F3...  56.3 us
    unnamed x4, local copies, waits for them, and re-layouts  2.13 us

profile of v3, /device:TPU:6, one launch (start us, length us, event | category | flops | bytes accessed | tf_op | source)
XLA Modules:
  0.0 59.1 jit_solution(552992284947600226)
XLA Ops:
  0.6 56.3 %shard_map.158 = (f32[3,6912]{1,0:T(4,128)}, f32[1,256]{1,0:T(1,128)}) custom-call(f32[3,6912]{1,0:T(4,128)} %refs_0_.1, f32[3,6912]{1,0:T(4,128)} %refs_1_.1, f32[3,6912]{1,0:T(4,128)} %refs_2_.1, f32[3,6912]{1,0:T(4,128)} %refs_3_.1, f32[192,256]{1,0:T(8,128)} %refs_4_.1, f32[1,256]{1,0:T(1,128)} %bitcast.4, f32[192,192]{1,0:T(8,128)} %refs_6_.1, ...), custom_call_target="tpu_custom_call" | custom-call | tf_op jit(solution)/shard_map/pallas_call | solution.py:536
  56.9 0.0 copy-start
  56.9 1.6 %copy.19 = f32[3,6912]{1,0:T(4,128)} copy(f32[3,6912]{1,0:T(4,128)} %get-tuple-element.8) | data formatting | bytes 165888
  58.5 0.0 copy-done
  58.5 0.6 copy.20
Async XLA Ops:
  56.9 1.6 %copy-start = (f32[1,256]{1,0:T(1,128)S(1)}, f32[1,256]{1,0:T(1,128)}, u32[]{:S(2)}) copy-start(f32[1,256]{1,0:T(1,128)} %get-tuple-element.5) | copy-start | bytes 3076

commit v4 on v3

--- a/solution.py
+++ b/solution.py
@@ -1,3 +1,5 @@
+import functools
+
 import jax
 import jax.numpy as jnp
 from jax import lax
@@ -16,8 +18,7 @@
 EXT = 8960
 PAD_CODE = 16368
 RELAXATION = 0.7
-BUILD_FIRST = 4
-PRIMAL_CUTS = (0, 1, 3, 4)
+BUILD_FIRST = 2
 
 LANES = 128
 OWNED = NODES_DEV // LANES
@@ -261,18 +262,49 @@
         cell_rows[span, :] = rows
         cell_lanes[span, :] = lanes
         hang_hots[span, :] = jnp.where(rows == HANG_ROW, 1.0, 0.0)
+        return carry
+
+    lax.fori_loop(0, 8, build, 0)
+
+    def build_hots(block):
+        span = pl.ds(pl.multiple_of(block * 8, 8), 8)
+        rows, lanes = cell_rows[span, :], cell_lanes[span, :]
         for step in range(8):
             spot = pl.ds(step * 256, 256)
             lane_hots[block, :, spot] = one_hot(lanes[step : step + 1], LANES, BF16)
             row_hots[block, :, spot] = one_hot(rows[step : step + 1], STRIDE, BF16)
             ghost_hots[block, :, spot] = one_hot(rows[step : step + 1], GHOSTS, F32, STRIDE)
+
+    def gather_block(rows_of, base, out, block, blocks=1):
+        spots, spans = [], []
+        for step in range(blocks):
+            low = pl.multiple_of((block * blocks + step) * 8, 8)
+            for half in range(2):
+                lane = pl.ds(half * LANES, LANES)
+                spots.append((cell_rows[pl.ds(low, 8), lane], cell_lanes[pl.ds(low, 8), lane]))
+                spans.append((low, lane))
+
+        def span(part, where):
+            return pl.ds(pl.multiple_of(part * 64 + where[0], 8), 8), where[1]
+
+        start = None
+        if base is not None:
+            start = [[base[span(part, where)] for part in range(3)] for where in spans]
+        found = looked_up(rows_of, spots, 3, start)
+        for values, where in zip(found, spans):
+            for part in range(3):
+                out[span(part, where)] = values[part]
+
+    def build_and_gather(block, carry):
+        build_hots(block)
+        gather_block(owned_rows(table), None, owned_cells, block)
         return carry
 
-    lax.fori_loop(0, BUILD_FIRST, build, 0)
+    lax.fori_loop(0, BUILD_FIRST, build_and_gather, 0)
     peers = jnp.minimum(me, REACH) + jnp.minimum(count - 1 - me, REACH)
     pl.semaphore_wait(barrier, peers)
     pending = exchange(send_first, recv_first, 0, 1)
-    lax.fori_loop(BUILD_FIRST, 8, build, 0)
+    lax.fori_loop(BUILD_FIRST, 8, build_and_gather, 0)
 
     hang_ids = lax.broadcasted_iota(jnp.int32, (16, LANES), 1)
     rows, lanes = place(modulo(17 * master_ref[...] + 8 * hang_ids, EXT))
@@ -295,29 +327,12 @@
     def hang_rows(values):
         return [(HANG_ROW, lambda part: values[part])]
 
-    def gather_cells(rows_of, base, out, first, end):
+    def gather_cells(rows_of, base, out, blocks):
         def body(group, carry):
-            spots, spans = [], []
-            for block in range(2):
-                for half in range(2):
-                    low = pl.multiple_of(group * 16 + block * 8, 8)
-                    lane = pl.ds(half * LANES, LANES)
-                    spots.append((cell_rows[pl.ds(low, 8), lane], cell_lanes[pl.ds(low, 8), lane]))
-                    spans.append((low, lane))
-
-            def span(part, where):
-                return pl.ds(pl.multiple_of(part * 64 + where[0], 8), 8), where[1]
-
-            start = None
-            if base is not None:
-                start = [[base[span(part, where)] for part in range(3)] for where in spans]
-            found = looked_up(rows_of, spots, 3, start)
-            for values, where in zip(found, spans):
-                for part in range(3):
-                    out[span(part, where)] = values[part]
+            gather_block(rows_of, base, out, group, blocks)
             return carry
 
-        lax.fori_loop(first, end, body, 0)
+        lax.fori_loop(0, 8 // blocks, body, 0)
 
     def image_rows(block):
         return [
@@ -348,8 +363,10 @@
         zero = jnp.zeros((2 * (3 * GHOSTS + 8), LANES), F32)
         return joined(lax.fori_loop(0, 8, body, zero))
 
-    def scatter_owned():
+    def scatter_owned(beside=None):
         def body(block, total):
+            if beside is not None:
+                beside(block)
             columns = []
             rows = image_rows(block)
             high = [each.astype(BF16).astype(F32) for each in rows]
@@ -379,7 +396,6 @@
         return form(stiff_high, high) + form(stiff_high, low) + form(stiff_low, high)
 
     owned_masters = looked_up(owned_rows(table), master_spots, 3)
-    gather_cells(owned_rows(table), None, owned_cells, 0, 4)
     for k in (1, 2, 6, 5):
         loads[k].wait()
     stiff = stiff_ref[...]
@@ -398,7 +414,7 @@
     for sweep in range(SWEEPS):
         finish(pending)
         hung = hanging(looked_up(ghost_rows(recv), master_spots, 3, owned_masters))
-        gather_cells(ghost_rows(recv) + hang_rows(hung), owned_cells, cells, 0, 4)
+        gather_cells(ghost_rows(recv) + hang_rows(hung), owned_cells, cells, 4)
         image[...] = modulus * product(cells[...], dot_tn)
         totals = scatter_ghosts()
         held = [
@@ -413,10 +429,12 @@
                 send[slot, 2 * part : 2 * part + 2, :] = totals[spot : spot + 2]
         pending = exchange(send, recv, 2 * sweep + 1, -1)
 
-        totals = scatter_owned() + released(held, 0, STRIDE)
+        beside = None
         if sweep == 0:
             primal_rows = owned_rows(primal_table) + ghost_rows(recv_first, 3)
             primal_rows += hang_rows(hanging(looked_up(primal_rows, master_spots, 3)))
+            beside = functools.partial(gather_block, primal_rows, None, primal_cells)
+        totals = scatter_owned(beside) + released(held, 0, STRIDE)
         if sweep == SWEEPS - 1:
             primal_cells[...] = modulus * product(primal_cells[...], dot)
             for k in (12, 13, 14):
@@ -425,10 +443,6 @@
                 owner_lanes[:, pl.ds(slot * LANES, LANES)] = one_hot(
                     sub_owner_ref[slot : slot + 1, :], 256, BF16
                 )
-        else:
-            gather_cells(
-                primal_rows, None, primal_cells, PRIMAL_CUTS[2 * sweep], PRIMAL_CUTS[2 * sweep + 1]
-            )
         finish(pending)
         columns = []
         for slot in range(SLOTS):
@@ -449,9 +463,7 @@
         pending = exchange(send, recv, 2 * sweep + 2, 1)
 
         owned_masters = looked_up(owned_rows(table), master_spots, 3)
-        gather_cells(owned_rows(table), None, owned_cells, 0, 4)
-        if sweep == 0:
-            gather_cells(primal_rows, None, primal_cells, PRIMAL_CUTS[1], 4)
+        gather_cells(owned_rows(table), None, owned_cells, 2)
 
     for part in range(3):
         for row in range(OWNED):
@@ -471,7 +483,7 @@
 
     finish(pending)
     hung = hanging(looked_up(ghost_rows(recv), master_spots, 3, owned_masters))
-    gather_cells(ghost_rows(recv) + hang_rows(hung), owned_cells, cells, 0, 4)
+    gather_cells(ghost_rows(recv) + hang_rows(hung), owned_cells, cells, 4)
     applied = primal_cells[...]
     work = applied * cells[...]
     work_high = work.astype(BF16)

time: 59.2 us -> 57.6 us (0.973)
  Pallas kernels: 56.3 us -> 54.7 us
    pallas_call x1, Pallas kernels: 56.3 us -> 54.7 us  [local(): pl.pallas_call(kernel, out_shape=(jax.ShapeDtypeStruct((3, NODES_DEV), F3...]
where the time goes in v4:
time: 57.6 us; the launch traced here: 57.5 us
  Pallas kernels  54.7 us (95%)
  local copies, waits for them, and re-layouts  2.13 us (4%)
  between operations  0.65 us (1%)
    pallas_call x1, Pallas kernels, local(): pl.pallas_call(kernel, out_shape=(jax.ShapeDtypeStruct((3, NODES_DEV), F3...  54.7 us
    unnamed x4, local copies, waits for them, and re-layouts  2.13 us

profile of v4, /device:TPU:6, one launch (start us, length us, event | category | flops | bytes accessed | tf_op | source)
XLA Modules:
  0.0 57.5 jit_solution(9183089104785167530)
XLA Ops:
  0.6 54.7 %shard_map.158 = (f32[3,6912]{1,0:T(4,128)}, f32[1,256]{1,0:T(1,128)}) custom-call(f32[3,6912]{1,0:T(4,128)} %refs_0_.1, f32[3,6912]{1,0:T(4,128)} %refs_1_.1, f32[3,6912]{1,0:T(4,128)} %refs_2_.1, f32[3,6912]{1,0:T(4,128)} %refs_3_.1, f32[192,256]{1,0:T(8,128)} %refs_4_.1, f32[1,256]{1,0:T(1,128)} %bitcast.4, f32[192,192]{1,0:T(8,128)} %refs_6_.1, ...), custom_call_target="tpu_custom_call" | custom-call | tf_op jit(solution)/shard_map/pallas_call | solution.py:548
  55.3 0.0 copy-start
  55.3 1.6 %copy.19 = f32[3,6912]{1,0:T(4,128)} copy(f32[3,6912]{1,0:T(4,128)} %get-tuple-element.8) | data formatting | bytes 165888
  56.9 0.0 copy-done
  56.9 0.6 copy.20
Async XLA Ops:
  55.3 1.6 %copy-start = (f32[1,256]{1,0:T(1,128)S(1)}, f32[1,256]{1,0:T(1,128)}, u32[]{:S(2)}) copy-start(f32[1,256]{1,0:T(1,128)} %get-tuple-element.5) | copy-start | bytes 3076

commit v5 on v4

--- a/solution.py
+++ b/solution.py
@@ -18,7 +18,7 @@
 EXT = 8960
 PAD_CODE = 16368
 RELAXATION = 0.7
-BUILD_FIRST = 2
+BUILD_FIRST = 0
 
 LANES = 128
 OWNED = NODES_DEV // LANES
@@ -26,6 +26,7 @@
 STRIDE = 64
 GHOSTS = 2 * SLOTS
 OFFSETS = [step + 1 for step in range(REACH)] + [-(step + 1) for step in range(REACH)]
+FAR_FIRST = sorted(range(SLOTS), key=lambda slot: -abs(OFFSETS[slot]))
 
 
 def modulo(values, divisor):
@@ -76,6 +77,19 @@
                 value = jnp.take_along_axis(table, lanes, axis=1, mode="promise_in_bounds")
                 each[part] = jnp.where(hit, value, each[part])
     return found
+
+
+def split_rows(rows):
+    high = [each.astype(BF16).astype(F32) for each in rows]
+    return high + [a - b for a, b in zip(rows, high)]
+
+
+def spread_whole(values, row_hot):
+    column = []
+    for each in values:
+        tile = jnp.broadcast_to(each, (16, each.shape[1])).astype(BF16)
+        column.append(row_hot * jnp.concatenate([tile] * (STRIDE // 16), 0))
+    return jnp.concatenate(column, 0)
 
 
 def spread(values, row_hot):
@@ -157,10 +171,12 @@
 
     sent = []
 
-    def exchange(send, recv, turn, direction):
+    def exchange(send, recv, turn, direction, ready=None):
         copies = []
-        for slot, offset in enumerate(OFFSETS):
-            away = direction * offset
+        for slot in FAR_FIRST:
+            if ready is not None:
+                ready(slot)
+            away = direction * OFFSETS[slot]
             copy = pltpu.make_async_remote_copy(
                 src_ref=send.at[slot],
                 dst_ref=recv.at[slot],
@@ -369,16 +385,14 @@
                 beside(block)
             columns = []
             rows = image_rows(block)
-            high = [each.astype(BF16).astype(F32) for each in rows]
-            values = high + [a - b for a, b in zip(rows, high)]
+            values = split_rows(rows)
             for step in range(8):
                 spot = pl.ds(step * 256, 256)
-                row_hot = row_hots[block, :, spot]
-                column = []
-                for each in values:
-                    tile = jnp.broadcast_to(each[step : step + 1], (16, 256)).astype(BF16)
-                    column.append(row_hot * jnp.concatenate([tile] * (STRIDE // 16), 0))
-                columns.append(jnp.concatenate(column, 0))
+                columns.append(
+                    spread_whole(
+                        [each[step : step + 1] for each in values], row_hots[block, :, spot]
+                    )
+                )
             return total + dot_nt(jnp.concatenate(columns, 1), lane_hots[block])
 
         return joined(lax.fori_loop(0, 8, body, jnp.zeros((6 * STRIDE, LANES), F32)))
@@ -408,13 +422,13 @@
         row = lists[slot : slot + 1]
         spot = pl.ds(slot * 256, 256)
         list_lanes[:, spot] = one_hot(row & 127, LANES, BF16)
-        list_hots[:, spot] = one_hot(row >> 7, STRIDE, F32)
+        list_hots[:, spot] = one_hot(row >> 7, STRIDE, BF16)
 
     recv, first = recv_first, 0
     for sweep in range(SWEEPS):
         finish(pending)
         hung = hanging(looked_up(ghost_rows(recv), master_spots, 3, owned_masters))
-        gather_cells(ghost_rows(recv) + hang_rows(hung), owned_cells, cells, 4)
+        gather_cells(ghost_rows(recv) + hang_rows(hung), owned_cells, cells, 8)
         image[...] = modulus * product(cells[...], dot_tn)
         totals = scatter_ghosts()
         held = [
@@ -423,11 +437,13 @@
         ]
         totals = totals[: 3 * GHOSTS] + released(held, STRIDE, GHOSTS)
         send, recv = send_ghost.at[2 * sweep], recv_ghost.at[2 * sweep]
-        for slot in range(SLOTS):
+
+        def ready(slot, send=send, totals=totals):
             for part in range(3):
                 spot = part * GHOSTS + 2 * slot
                 send[slot, 2 * part : 2 * part + 2, :] = totals[spot : spot + 2]
-        pending = exchange(send, recv, 2 * sweep + 1, -1)
+
+        pending = exchange(send, recv, 2 * sweep + 1, -1, ready)
 
         beside = None
         if sweep == 0:
@@ -453,7 +469,9 @@
                 )
                 for part in range(3)
             ]
-            columns.append(spread(rows, list_hots[:, pl.ds(slot * 256, 256)]))
+            columns.append(
+                spread_whole(split_rows(rows), list_hots[:, pl.ds(slot * 256, 256)])
+            )
         returned = joined(dot_nt(jnp.concatenate(columns, 1), list_lanes[...]))
         table[...] = table[...] + RELAXATION * inverse[...] * (
             source[...] - (totals + returned)
@@ -483,7 +501,7 @@
 
     finish(pending)
     hung = hanging(looked_up(ghost_rows(recv), master_spots, 3, owned_masters))
-    gather_cells(ghost_rows(recv) + hang_rows(hung), owned_cells, cells, 4)
+    gather_cells(ghost_rows(recv) + hang_rows(hung), owned_cells, cells, 8)
     applied = primal_cells[...]
     work = applied * cells[...]
     work_high = work.astype(BF16)
@@ -565,7 +583,7 @@
             vmem((8, LANES, 8 * 256), BF16),
             vmem((64, 256), jnp.int32),
             vmem((64, 256), jnp.int32),
-            vmem((STRIDE, SLOTS * 256), F32),
+            vmem((STRIDE, SLOTS * 256), BF16),
             vmem((LANES, SLOTS * 256), BF16),
             vmem((STRIDE + GHOSTS, 16 * LANES), F32),
             vmem((LANES, 16 * LANES), BF16),

time: 57.6 us -> 57.4 us (level)
  no operation moved by 1% of the time
where the time goes in v5:
time: 57.4 us; the launch traced here: 57.3 us
  Pallas kernels  54.5 us (95%)
  local copies, waits for them, and re-layouts  2.13 us (4%)
  between operations  0.65 us (1%)
    pallas_call x1, Pallas kernels, local(): pl.pallas_call(kernel, out_shape=(jax.ShapeDtypeStruct((3, NODES_DEV), F3...  54.5 us
    unnamed x4, local copies, waits for them, and re-layouts  2.13 us

profile of v5, /device:TPU:6, one launch (start us, length us, event | category | flops | bytes accessed | tf_op | source)
XLA Modules:
  0.0 57.3 jit_solution(4427348758142348039)
XLA Ops:
  0.6 54.5 %shard_map.158 = (f32[3,6912]{1,0:T(4,128)}, f32[1,256]{1,0:T(1,128)}) custom-call(f32[3,6912]{1,0:T(4,128)} %refs_0_.1, f32[3,6912]{1,0:T(4,128)} %refs_1_.1, f32[3,6912]{1,0:T(4,128)} %refs_2_.1, f32[3,6912]{1,0:T(4,128)} %refs_3_.1, f32[192,256]{1,0:T(8,128)} %refs_4_.1, f32[1,256]{1,0:T(1,128)} %bitcast.4, f32[192,192]{1,0:T(8,128)} %refs_6_.1, ...), custom_call_target="tpu_custom_call" | custom-call | tf_op jit(solution)/shard_map/pallas_call | solution.py:566
  55.1 0.0 copy-start
  55.1 1.6 %copy.19 = f32[3,6912]{1,0:T(4,128)} copy(f32[3,6912]{1,0:T(4,128)} %get-tuple-element.8) | data formatting | bytes 165888
  56.7 0.0 copy-done
  56.7 0.6 copy.20
Async XLA Ops:
  55.1 1.6 %copy-start = (f32[1,256]{1,0:T(1,128)S(1)}, f32[1,256]{1,0:T(1,128)}, u32[]{:S(2)}) copy-start(f32[1,256]{1,0:T(1,128)} %get-tuple-element.5) | copy-start | bytes 3076
